TPU v7x, 512 devices: a whole 4x8x8 slice. The times are simulated.
512 devices in a mesh: ctx: 64 (over z_hi, y, core), tp: 8 (over x, z_lo).
Axes of the slice: x: 4, y: 8, z: 8 (z_hi: 4, z_lo: 2; z = z_hi * 2 + z_lo), core: 2. Of those that a mesh axis runs over, the one named last changes fastest.
Arguments:
- x_stash: bfloat16 [8192, 4096], P('ctx', 'tp'), may hold values from -6 to 6
- w_key: bfloat16 [4096, 1024], P(None, 'tp'), may hold values from -0.09375 to 0.09375
- w_value: bfloat16 [4096, 1024], P(None, 'tp'), may hold values from -0.09375 to 0.09375
- query: bfloat16 [8192, 4096], P('ctx', 'tp'), may hold values from -64 to 64
- out_stash: bfloat16 [8192, 4096], P('ctx', 'tp'), may hold values from -6 to 6
- d_out: bfloat16 [8192, 4096], P('ctx', 'tp'), may hold values from -24 to 24
- roster: int32 [128], replicated, may hold values from 0 to 127, each once
Outputs:
- d_query: bfloat16 [8192, 4096], P('ctx', 'tp')
- d_input: bfloat16 [8192, 4096], P('ctx', 'tp')
Inputs may be any that keep to these rules, and one draw needn't show every extreme that they name: Every block index of the sequence appears once; stored rows r * 128 to r * 128 + 63 are block roster[2 r], the next 64 rows block roster[2 r + 1].
All inputs are finite; a program needn't handle non-finite values.
Results may differ from a plain program's by a relative error of at most 0.025.
The roundings to bfloat16 on the way count: a program that leaves them out, or rounds other values in their place, can miss the bound.
Values may be sent and summed in bfloat16 or wider, within the bound.
A program may use at most 64 MiB of HBM per device.

v0:
```python
import jax
import jax.numpy as jnp
from jax import lax
from jax.sharding import PartitionSpec as P

HD = 128


NEG_FILL = -1e30
ROPE_BASE = 500000.0


def shifted(value, axis, steps):
    count = lax.axis_size(axis)
    pairs = [(source, (source + steps) % count) for source in range(count)]
    return lax.ppermute(value, axis, pairs)


def row_positions(roster, first_row, row_count, block_rows):
    row_ids = first_row + jnp.arange(row_count, dtype=jnp.int32)
    blocks = jnp.take(roster, row_ids // block_rows)
    return blocks * block_rows + row_ids % block_rows


def rope_tables(positions, head_dim):
    half_dim = head_dim // 2
    frequency = ROPE_BASE ** (-(jnp.arange(half_dim, dtype=jnp.float32) * 2.0) / head_dim)
    angles = positions.astype(jnp.float32)[:, None, None] * frequency[None, None, :]
    return (jnp.cos(angles), jnp.sin(angles))


def rotate(tensor, cosine, sine_part, direction):
    half_dim = tensor.shape[-1] // 2
    first_half = tensor[..., :half_dim]
    second_half = tensor[..., half_dim:]
    return jnp.concatenate(
        [
            first_half * cosine - direction * second_half * sine_part,
            second_half * cosine + direction * first_half * sine_part,
        ],
        axis=-1,
    )


def body(x_stash, w_key, w_value, query, out_stash, d_out, roster):
    tok_rows = x_stash.shape[0]
    head_dim = HD
    kv_local = w_key.shape[1] // head_dim
    group_size = query.shape[1] // (kv_local * head_dim)
    block_rows = tok_rows // 2
    cycle_size = lax.axis_size("ctx")
    cycle_rank = lax.axis_index("ctx")
    score_scale = head_dim ** (-0.5)
    zero_kv = jnp.zeros((tok_rows, kv_local * head_dim), jnp.float32)
    received = lax.all_gather(x_stash, "tp", axis=1, tiled=True)
    key_raw = jnp.dot(received, w_key, preferred_element_type=jnp.float32)
    value_raw = jnp.dot(received, w_value, preferred_element_type=jnp.float32)
    my_pos = row_positions(roster, cycle_rank * tok_rows, tok_rows, block_rows)
    cosine, sine_part = rope_tables(my_pos, head_dim)
    own_keys = rotate(key_raw.reshape(tok_rows, kv_local, head_dim), cosine, sine_part, 1.0)
    own_keys = own_keys.astype(jnp.bfloat16).reshape(tok_rows, kv_local * head_dim)
    own_values = value_raw.astype(jnp.bfloat16)
    query_heads = query.reshape(tok_rows, kv_local, group_size, head_dim)
    grad_heads = d_out.reshape(tok_rows, kv_local, group_size, head_dim)
    out_heads = out_stash.reshape(tok_rows, kv_local, group_size, head_dim)
    delta = jnp.einsum(
        "tkgd,tkgd->kgt", grad_heads.astype(jnp.float32), out_heads.astype(jnp.float32)
    )

    def key_scores(key_block):
        key_heads = key_block.reshape(-1, kv_local, head_dim)
        return (
            jnp.einsum("tkgd,skd->kgts", query_heads, key_heads, preferred_element_type=jnp.float32)
            * score_scale
        )

    def stats_block(running, key_block, first_row):
        row_peak, exp_total = running
        key_pos = row_positions(roster, first_row, key_block.shape[0], block_rows)
        allowed = key_pos[None, :] <= my_pos[:, None]
        scores = jnp.where(allowed, key_scores(key_block), NEG_FILL)
        new_peak = jnp.maximum(row_peak, jnp.max(scores, axis=-1))
        weights = jnp.where(allowed, jnp.exp(scores - new_peak[..., None]), 0.0)
        return (new_peak, exp_total * jnp.exp(row_peak - new_peak) + jnp.sum(weights, axis=-1))

    stats_start = (
        jnp.full((kv_local, group_size, tok_rows), NEG_FILL, jnp.float32),
        jnp.zeros((kv_local, group_size, tok_rows), jnp.float32),
    )
    received = lax.all_gather(own_keys, "ctx", axis=0, tiled=True)
    row_count = received.shape[0]
    step_rows = min(row_count, tok_rows)

    def one_block(block_index, inner_acc):
        offset = block_index * step_rows
        return stats_block(
            inner_acc, lax.dynamic_slice_in_dim(received, offset, step_rows, 0), offset
        )

    folded = lax.fori_loop(0, row_count // step_rows, one_block, stats_start)
    row_peak, exp_total = (folded[0], folded[1])
    log_total = row_peak + jnp.log(exp_total)

    def attend(key_block, value_block, key_pos, running):
        d_query, grad_k, grad_v = running
        allowed = key_pos[None, :] <= my_pos[:, None]
        key_heads = key_block.reshape(tok_rows, kv_local, head_dim)
        value_heads = value_block.reshape(tok_rows, kv_local, head_dim)
        probs_f = jnp.where(allowed, jnp.exp(key_scores(key_block) - log_total[..., None]), 0.0)
        probs_b = probs_f.astype(jnp.bfloat16)
        value_term = jnp.einsum(
            "kgts,tkgd->skd", probs_b, grad_heads, preferred_element_type=jnp.float32
        )
        d_probs = jnp.einsum(
            "tkgd,skd->kgts", grad_heads, value_heads, preferred_element_type=jnp.float32
        )
        d_scores = (probs_f * (d_probs - delta[..., None])).astype(jnp.bfloat16)
        d_query = (
            d_query
            + jnp.einsum("kgts,skd->tkgd", d_scores, key_heads, preferred_element_type=jnp.float32)
            * score_scale
        )
        key_term = (
            jnp.einsum("kgts,tkgd->skd", d_scores, query_heads, preferred_element_type=jnp.float32)
            * score_scale
        )
        grad_k = grad_k + key_term.reshape(tok_rows, kv_local * head_dim)
        grad_v = grad_v + value_term.reshape(tok_rows, kv_local * head_dim)
        return (d_query, grad_k, grad_v)

    def visit(key_block, value_block, anchor, running):
        key_pos = row_positions(roster, anchor * tok_rows, tok_rows, block_rows)
        return attend(key_block, value_block, key_pos, running)

    zero_query = jnp.zeros((tok_rows, kv_local, group_size, head_dim), jnp.float32)
    d_query, grad_k, grad_v = visit(
        own_keys, own_values, cycle_rank, (zero_query, zero_kv, zero_kv)
    )

    def cycle_turn(turn_index, loop_state):
        keys_c, values_c, d_query, grad_kc, grad_vc = loop_state
        keys_c, values_c = shifted((keys_c, values_c), "ctx", 1)
        grad_kc, grad_vc = shifted((grad_kc, grad_vc), "ctx", 1)
        d_query, grad_kc, grad_vc = visit(
            keys_c, values_c, (cycle_rank - turn_index) % cycle_size, (d_query, grad_kc, grad_vc)
        )
        return (keys_c, values_c, d_query, grad_kc, grad_vc)

    loop_state = lax.fori_loop(
        1, cycle_size, cycle_turn, (own_keys, own_values, d_query, grad_k, grad_v)
    )
    d_query = loop_state[2]
    grad_k, grad_v = (
        shifted(loop_state[3].astype(jnp.bfloat16), "ctx", 1).astype(jnp.float32),
        shifted(loop_state[4].astype(jnp.bfloat16), "ctx", 1).astype(jnp.float32),
    )
    d_key = rotate(grad_k.reshape(tok_rows, kv_local, head_dim), cosine, sine_part, -1.0)
    d_key = d_key.astype(jnp.bfloat16).reshape(tok_rows, kv_local * head_dim)
    d_value = grad_v.astype(jnp.bfloat16)
    partial_sum = jnp.einsum("tc,dc->td", d_key, w_key, preferred_element_type=jnp.float32)
    partial_sum = partial_sum + jnp.einsum(
        "tc,dc->td", d_value, w_value, preferred_element_type=jnp.float32
    )
    d_input = lax.psum_scatter(
        partial_sum.astype(jnp.bfloat16), "tp", scatter_dimension=1, tiled=True
    )
    d_query_out = d_query.astype(jnp.bfloat16).reshape(tok_rows, kv_local * group_size * head_dim)
    return (d_query_out, d_input)


def solution(mesh):
    in_specs = (
        P("ctx", "tp"),
        P(None, "tp"),
        P(None, "tp"),
        P("ctx", "tp"),
        P("ctx", "tp"),
        P("ctx", "tp"),
        P(),
    )
    out_specs = (P("ctx", "tp"), P("ctx", "tp"))
    return jax.shard_map(body, mesh=mesh, in_specs=in_specs, out_specs=out_specs, check_vma=False)
```

profile of v0, /device:TPU:1, one launch (start us, length us, event | category | flops | bytes accessed | tf_op | source)
XLA Modules:
  0.0 1449.3 jit_solution(11834048811455966499)
XLA Ops:
  9.7 47.4 %all-gather.3.cloned.1.call-done = bf16[128,4096]{1,0:T(8,128)(2,1)} async-done(((bf16[128,512]{1,0:T(8,128)(2,1)}), bf16[128,4096]{1,0:T(8,128)(2,1)}) %all-gather.3.cloned.1.call-update) | async-done | bytes 1048592 | tf_op jit(solution)/shard_map/all_gather | solution.py:55
  70.2 76.8 %all-gather.5.cloned.1.call-done = bf16[8192,128]{0,1:T(8,128)(2,1)} async-done(((bf16[128,128]{0,1:T(8,128)(2,1)}), bf16[8192,128]{0,1:T(8,128)(2,1)}) %all-gather.5.cloned.1.call-update) | async-done | bytes 2097168 | tf_op jit(solution)/shard_map/all_gather | solution.py:90
  147.0 239.2 %while.42 = (s32[]{:T(128)}, f32[1,4,128]{2,1,0:T(4,128)S(1)}, f32[1,4,128]{2,1,0:T(4,128)}, s32[128]{0:T(128)S(1)}, s32[128]{0:T(128)S(1)}, /*index=5*/bf16[819...) while((s32[]{:T(128)}, f32[1,4,128]{2,1,0:T(4,128)S(1)}, ...), condition=%wide.region_3.5_spmd.clone, body=%wide.region_0.4_spmd.clone.sunk | while | flops 17196548 | bytes 772794 | solution.py:100
  388.0 999.8 %while.41 = (s32[]{:T(128)}, bf16[128,128]{1,0:T(8,128)(2,1)S(1)}, bf16[128,128]{1,0:T(8,128)(2,1)S(1)}, f32[128,1,4,128]{3,0,2,1:T(8,128)S(1)}, f32[128,128]{1,...) while((s32[]{:T(128)}, bf16[128,128]{1,0:T(8,128)(2,1)S(1)}, ...), condition=%wide.region_5.7_spmd, body=%wide.region_4.6_spmd.sunk | while | flops 84548624 | bytes 3552210 | solution.py:149
  392.5 3.3 collective-permute-start.3
  400.5 3.3 collective-permute-start.1
  405.7 3.2 collective-permute-start.3
  418.6 4.5 collective-permute-start.3
  471.1 2.7 collective-permute-done
  487.1 2.7 collective-permute-done
  503.0 2.7 collective-permute-done
  518.9 2.7 collective-permute-done
  534.9 2.9 collective-permute-done
  551.0 2.8 collective-permute-done
  567.0 2.9 collective-permute-done
  583.1 2.9 collective-permute-done
  599.2 2.9 collective-permute-done
  615.3 2.9 collective-permute-done
  631.5 2.9 collective-permute-done
  679.2 2.8 collective-permute-done
  695.2 2.9 collective-permute-done
  758.9 2.9 collective-permute-done
  775.0 2.7 collective-permute-done
  822.8 2.8 collective-permute-done
  838.8 2.7 collective-permute-done
  854.7 2.7 collective-permute-done
  886.6 2.9 collective-permute-done
  902.7 2.9 collective-permute-done
  934.7 2.7 collective-permute-done
  966.4 2.9 collective-permute-done
  982.5 2.7 collective-permute-done
  1030.3 2.8 collective-permute-done
  1046.3 2.7 collective-permute-done
  1094.0 2.8 collective-permute-done
  1110.0 2.7 collective-permute-done
  1125.9 2.7 collective-permute-done
  1157.8 2.9 collective-permute-done
  1189.8 2.7 collective-permute-done
  1221.6 2.8 collective-permute-done
  1237.6 2.7 collective-permute-done
  1285.4 2.8 collective-permute-done
  1301.4 2.7 collective-permute-done
  1317.3 2.7 collective-permute-done
  1349.1 2.8 collective-permute-done
  1365.1 2.7 collective-permute-done
  1381.0 2.7 collective-permute-done
  1391.8 6.1 collective-permute-done.4
  1402.2 40.5 %reduce-scatter.2.cloned.1.call-done = bf16[128,512]{1,0:T(8,128)(2,1)} async-done(((bf16[128,4096]{1,0:T(8,128)(2,1)}), bf16[128,512]{1,0:T(8,128)(2,1)}) %reduce-scatter.2.cloned.1.call-update) | async-done | bytes 131088 | tf_op jit(solution)/shard_map/reduce_scatter | solution.py:164
  (1940 shorter events, 1131.6 us)
Async XLA Ops:
  7.2 49.9 %all-gather.3.cloned.1.call-start = ((), (), s32[]{:S(2)}) async-start(), calls=%async_computation.1 | async-start | bytes 1179648 | tf_op jit(solution)/shard_map/all_gather | solution.py:55
  7.9 139.0 %all-gather.5.cloned.1.call-start = ((), (), s32[]{:S(2)}) async-start(), calls=%async_computation.2 | async-start | bytes 2129920 | tf_op jit(solution)/shard_map/all_gather | solution.py:90
  59.8 1382.9 %reduce-scatter.2.cloned.1.call-start = ((), (), s32[]{:S(2)}) async-start(), calls=%async_computation.3 | async-start | bytes 1179648 | tf_op jit(solution)/shard_map/reduce_scatter | solution.py:164
  414.1 12.5 collective-permute-start.1
  430.1 12.1 collective-permute-start.1
  446.1 12.1 collective-permute-start.1
  462.0 12.1 collective-permute-start.1
  477.9 12.1 collective-permute-start.1
  493.9 12.1 collective-permute-start.1
  509.8 12.1 collective-permute-start.1
  525.7 12.3 collective-permute-start.1
  541.9 12.1 collective-permute-start.1
  557.9 12.2 collective-permute-start.1
  574.0 12.3 collective-permute-start.1
  590.1 12.3 collective-permute-start.1
  606.2 12.3 collective-permute-start.1
  622.4 12.2 collective-permute-start.1
  670.1 12.1 collective-permute-start.1
  686.1 12.3 collective-permute-start.1
  702.2 12.0 collective-permute-start.1
  749.8 12.3 collective-permute-start.1
  765.9 12.1 collective-permute-start.1
  781.9 12.0 collective-permute-start.1
  813.6 12.1 collective-permute-start.1
  829.7 12.1 collective-permute-start.1
  845.6 12.0 collective-permute-start.1
  877.5 12.2 collective-permute-start.1
  893.5 12.2 collective-permute-start.1
  925.6 12.0 collective-permute-start.1
  957.3 12.2 collective-permute-start.1
  973.4 12.0 collective-permute-start.1
  1021.2 12.1 collective-permute-start.1
  1037.2 12.0 collective-permute-start.1
  1069.0 12.0 collective-permute-start.1
  1084.9 12.1 collective-permute-start.1
  1100.9 12.0 collective-permute-start.1
  1116.8 12.0 collective-permute-start.1
  1148.7 12.2 collective-permute-start.1
  1180.7 12.0 collective-permute-start.1
  1212.5 12.1 collective-permute-start.1
  1228.5 12.0 collective-permute-start.1
  1260.3 12.0 collective-permute-start.1
  1276.3 12.1 collective-permute-start.1
  1292.2 12.0 collective-permute-start.1
  1308.2 12.0 collective-permute-start.1
  1340.0 12.1 collective-permute-start.1
  1356.0 12.0 collective-permute-start.1
  1371.9 12.0 collective-permute-start.1
  (227 other events, 5740.3 us)
Sparse Core Ops, SparseCore 0:
  10.1 46.9 all-gather.2
  60.2 86.6 all-gather.4
  1401.5 41.1 reduce-scatter.1
where the time goes:
time: 1470 us; the launch traced here: 1450 us
  waiting for transfers between devices  522 us (36%)
  starting transfers between devices  498 us (34%)
  local copies, waits for them, and re-layouts  166 us (11%)
  matrix products  131 us (9%)
  other arithmetic  107 us (7%)
    ppermute x254, starting transfers between devices, shifted(): return lax.ppermute(value, axis, pairs)  497 us
    ppermute x254, waiting for transfers between devices, shifted(): return lax.ppermute(value, axis, pairs)  356 us
    gather x128, local copies, waits for them, and re-layouts, row_positions(): blocks = jnp.take(roster, row_ids // block_rows)  157 us
    add x64, other arithmetic, stats_block(): exp_total * jnp.exp(row_peak - new_peak) + jnp.sum(weights, axis=-1)  82.2 us
    all_gather x1, waiting for transfers between devices, body(): received = lax.all_gather(own_keys, 'ctx', axis=0, tiled=True)  76.8 us
    dot_general x128, matrix products, key_scores(): jnp.einsum('tkgd,skd->kgts', query_heads, key_heads, preferred_element_ty...  76.6 us
    all_gather x1, waiting for transfers between devices, body(): received = lax.all_gather(x_stash, 'tp', axis=1, tiled=True)  47.4 us
    reduce_scatter x1, waiting for transfers between devices, body(): lax.psum_scatter(partial_sum.astype(jnp.bfloat16), 'tp', scatter_dimensio...  40.5 us
  transfers between devices with their start and end apart: 257, of which 188 were waited for; matrix products, arithmetic and copies ran while one was open for 10% of the time, Pallas kernels for 0%

commit v1 on v0

v1 whole, which is shorter than its diff:
```python
import functools

import jax
import jax.numpy as jnp
import numpy as np
from jax import lax
from jax.experimental import pallas as pl
from jax.experimental.pallas import tpu as pltpu
from jax.sharding import PartitionSpec as P

HD = 128
GROUP = 4
BLOCK = 64
ROWS = 128
WIDE = GROUP * HD
ROPE_BASE = 500000.0
SCALE = HD ** -0.5
LOG2E = 1.4426950408889634
NEG = -1e30
FLOOR = -1e20

GRIDS = {(64, 8): (4, 8, 4, 2)}

NT = (((1,), (1,)), ((), ()))


def matmul_nt(a, b):
    return lax.dot_general(a, b, NT, preferred_element_type=jnp.float32)


def matmul(a, b):
    return jnp.dot(a, b, preferred_element_type=jnp.float32)


def stacked(block):
    return jnp.concatenate([block[:, h * HD:(h + 1) * HD] for h in range(GROUP)], axis=0)


def far_first(count):
    return sorted(range(count), key=lambda d: (-min(d, count - d), d))


def near_first(count):
    return sorted(range(1, count), key=lambda d: (min(d, count - d), d))


def kernel(
    grid, x_in, wk_in, wv_in, q_in, o_in, g_in, roster, freq,
    dq_out, di_out,
    xg, wkv, qg, gg, ol, kv, kt, posk, posq, probs, peak, total, fac, lse_own, lse_got,
    delta, dqt, dq_snd, dq_sib, dq_got, acc, dkv_snd, dkv_got, di_snd, di_got, dq_res, di_res,
    send_sem, recv_sem, local_sem,
):
    nz, ny, nx, nl = grid
    nj = 2 * nz
    chunks = ny // 2
    ctx, tp = lax.axis_index("ctx"), lax.axis_index("tp")
    z, y, c = ctx // (2 * ny), (ctx // 2) % ny, ctx % 2
    xi, zl = tp // nl, tp % nl

    def ctx_at(dz, dy, dc):
        return (((z + dz) % nz) * ny + (y + dy) % ny) * 2 + (c + dc) % 2

    def tp_at(dx, dl):
        return ((xi + dx) % nx) * nl + (zl + dl) % nl

    tp_peers = [(dx, dl) for dx in range(nx) for dl in range(nl) if (dx, dl) != (0, 0)]
    q_peers = [(dz, dc) for dz in range(nz) for dc in range(2) if (dz, dc) != (0, 0)]
    y_peers = list(range(1, ny))

    used = [0, 0]

    def local(src, dst):
        copy = pltpu.make_async_copy(src, dst, local_sem.at[used[0]])
        used[0] += 1
        copy.start()
        return copy

    sent = []

    def remote(src, dst, at_ctx, at_tp):
        i = used[1]
        used[1] += 1
        copy = pltpu.make_async_remote_copy(
            src_ref=src, dst_ref=dst, send_sem=send_sem.at[i], recv_sem=recv_sem.at[i],
            device_id=(at_ctx, at_tp), device_id_type=pl.DeviceIdType.MESH,
        )
        copy.start()
        sent.append(copy)
        return copy

    load_x = local(x_in, xg.at[0])
    load_wk = local(wk_in, wkv.at[:, 0:HD])
    load_wv = local(wv_in, wkv.at[:, HD:2 * HD])
    load_g = local(g_in, gg.at[0])
    load_o = local(o_in, ol)
    load_q = local(q_in, qg.at[0])

    barrier = pltpu.get_barrier_semaphore()
    partners = [(ctx, tp_at(dx, dl)) for dx, dl in tp_peers]
    partners += [(ctx_at(dz, 0, dc), tp) for dz, dc in q_peers]
    partners += [(ctx_at(0, dy, 0), tp) for dy in y_peers]
    for partner in partners:
        pl.semaphore_signal(barrier, inc=1, device_id=partner, device_id_type=pl.DeviceIdType.MESH)
    pl.semaphore_wait(barrier, len(partners))

    got_x = {}
    if nl > 1:
        got_x[0, 1] = remote(x_in, xg.at[1], ctx, tp_at(0, 1))
    for dx in near_first(nx):
        got_x[dx, 0] = remote(x_in, xg.at[dx * nl], ctx, tp_at(dx, 0))
    got_q = {}
    for dz in near_first(nz):
        got_q[dz, 0] = remote(q_in, qg.at[2 * dz], ctx_at(dz, 0, 0), tp)
    got_q[0, 1] = remote(q_in, qg.at[1], ctx_at(0, 0, 1), tp)

    order = far_first(ny)
    place = {dy: p for p, dy in enumerate(order)}
    row_id = lax.broadcasted_iota(jnp.int32, (ROWS, HD), 0)
    lane_id = lax.broadcasted_iota(jnp.int32, (1, ROWS), 1)
    for p, dy in enumerate(order):
        at = ctx_at(0, ny - dy, 0)
        first, second = roster[2 * at] * BLOCK, roster[2 * at + 1] * BLOCK
        posk[p * ROWS:(p + 1) * ROWS, :] = row_id + jnp.where(row_id < BLOCK, first, second - BLOCK)
    for j in range(nj):
        at = ctx_at(nz - j // 2, 0, 2 - j % 2)
        first, second = roster[2 * at] * BLOCK, roster[2 * at + 1] * BLOCK
        posq[j:j + 1, :] = lane_id + jnp.where(lane_id < BLOCK, first, second - BLOCK)
    own = place[0]
    angle = posk[own * ROWS:(own + 1) * ROWS, :].astype(jnp.float32) * freq[...]
    cosine = jnp.cos(angle)
    lane = lax.broadcasted_iota(jnp.int32, (ROWS, HD), 1)
    sine = jnp.where(lane < HD // 2, -1.0, 1.0) * jnp.sin(angle)

    load_g.wait()
    load_o.wait()
    for h in range(GROUP):
        cols = slice(h * HD, (h + 1) * HD)
        product = gg[0, :, cols].astype(jnp.float32) * ol[:, cols].astype(jnp.float32)
        delta[0, :, cols] = jnp.sum(product.T, axis=0, keepdims=True)

    def project(dx, dl):
        at = ((xi + nx - dx) % nx) * nl + (zl + nl - dl) % nl
        rows = pl.ds(pl.multiple_of(at * WIDE, WIDE), WIDE)
        return matmul(xg[dx * nl + dl], wkv[rows, :])

    load_x.wait()
    load_wk.wait()
    load_wv.wait()
    raw = project(0, 0)
    if nl > 1:
        got_x[0, 1].wait_recv()
        for dx in near_first(nx):
            got_x[dx, 1] = remote(xg.at[1], xg.at[dx * nl + 1], ctx, tp_at(dx, 0))
        raw += project(0, 1)
    for dx in near_first(nx):
        got_x[dx, 0].wait_recv()
        raw += project(dx, 0)
    got_g = {}
    for dz in near_first(nz):
        got_g[dz, 0] = remote(g_in, gg.at[2 * dz], ctx_at(dz, 0, 0), tp)
    got_g[0, 1] = remote(g_in, gg.at[1], ctx_at(0, 0, 1), tp)
    got_delta = [
        remote(delta.at[0], delta.at[2 * dz + dc], ctx_at(dz, 0, dc), tp) for dz, dc in q_peers
    ]
    for dz in near_first(nz):
        got_q[dz, 0].wait_recv()
        got_q[dz, 1] = remote(qg.at[2 * dz], qg.at[2 * dz + 1], ctx_at(0, 0, 1), tp)
    if nl > 1:
        for dx in near_first(nx):
            got_x[dx, 1].wait_recv()
            raw += project(dx, 1)
    key_raw = raw[:, 0:HD]
    keys = key_raw * cosine + pltpu.roll(key_raw, HD // 2, 1) * sine
    own_rows = pl.ds(own * ROWS, ROWS)
    kv[own_rows, 0:HD] = keys.astype(jnp.bfloat16)
    kv[own_rows, HD:2 * HD] = raw[:, HD:2 * HD].astype(jnp.bfloat16)
    got_kv = {}
    for dy in near_first(ny):
        got_kv[dy] = remote(
            kv.at[own_rows, :], kv.at[pl.ds(place[dy] * ROWS, ROWS), :], ctx_at(0, dy, 0), tp
        )
    load_q.wait()
    got_q[0, 1].wait_recv()
    for dz in near_first(nz):
        got_q[dz, 1].wait_recv()

    def table_row(j):
        at = ((z + nz - j // 2) % nz) * 2 + (c + 2 - j % 2) % 2
        return at

    for k in reversed(range(chunks)):
        for dy in order[2 * k:2 * k + 2]:
            if dy:
                got_kv[dy].wait_recv()
        rows = slice(2 * k * ROWS, 2 * (k + 1) * ROWS)
        kt[k] = kv[rows, 0:HD].astype(jnp.float32).T.astype(jnp.bfloat16)

        def score_step(j, carry, k=k, rows=rows):
            at = table_row(j)
            scores = matmul_nt(kv[rows, 0:HD], stacked(qg[j]))
            allowed = posk[rows, :] <= posq[pl.ds(j, 1), :]
            for h in range(GROUP):
                cols = slice(h * HD, (h + 1) * HD)
                part = jnp.where(allowed, scores[:, cols] * (SCALE * LOG2E), NEG)
                top = jnp.maximum(jnp.max(part, axis=0, keepdims=True), FLOOR)
                weight = jnp.exp2(part - top)
                probs[k, j, :, cols] = weight
                peak[k, at, :, cols] = top
                total[k, at, :, cols] = jnp.sum(weight, axis=0, keepdims=True)
            return carry

        lax.fori_loop(0, nj, score_step, 0)

    top = peak[0]
    for k in range(1, chunks):
        top = jnp.maximum(top, peak[k])
    mass = total[0] * jnp.exp2(peak[0] - top)
    for k in range(1, chunks):
        mass += total[k] * jnp.exp2(peak[k] - top)
    lse_own[...] = jnp.where(mass > 0.0, top + jnp.log(jnp.maximum(mass, 1e-30)) * LOG2E, NEG)
    got_lse = [
        remote(lse_own, lse_got.at[2 * dz + dc], ctx_at(dz, 0, dc), tp) for dz, dc in q_peers
    ]
    load_g_sib = got_g[0, 1]
    for dz in near_first(nz):
        got_g[dz, 0].wait_recv()
        got_g[dz, 1] = remote(gg.at[2 * dz], gg.at[2 * dz + 1], ctx_at(0, 0, 1), tp)
    for copy in got_lse:
        copy.wait_recv()
    top = lse_own[...]
    for s in range(1, nj):
        top = jnp.maximum(top, lse_got[s])
    mass = jnp.exp2(lse_own[...] - top)
    for s in range(1, nj):
        mass += jnp.exp2(lse_got[s] - top)
    lse = top + jnp.log(mass) * LOG2E
    for k in range(chunks):
        fac[k] = jnp.exp2(peak[k] - lse)
    for copy in got_delta:
        copy.wait_recv()
    load_g_sib.wait_recv()
    for dz in near_first(nz):
        got_g[dz, 1].wait_recv()

    got_dkv = {}
    got_sib = {}
    for k in range(chunks):
        rows = slice(2 * k * ROWS, 2 * (k + 1) * ROWS)
        acc[...] = jnp.zeros_like(acc)

        def grad_step(j, k=k, rows=rows):
            at = table_row(j)
            gs, qs = stacked(gg[j]), stacked(qg[j])
            d_probs = matmul_nt(kv[rows, HD:2 * HD], gs)
            prob = probs[k, j] * fac[k, at]
            d_scores = (prob * (d_probs - delta[j])).astype(jnp.bfloat16)
            acc[:, HD:2 * HD] += matmul(prob.astype(jnp.bfloat16), gs)
            acc[:, 0:HD] += matmul(d_scores, qs)
            part = matmul(kt[k], d_scores)
            if k == 0:
                dqt[j] = part
            else:
                dqt[j] += part

        def odd(i, carry, step=grad_step):
            step(2 * i + 1)
            return carry

        def even(i, carry, step=grad_step):
            step(2 * i)
            return carry

        def every(j, carry, step=grad_step):
            step(j)
            return carry

        if k < chunks - 1:
            lax.fori_loop(0, nj, every, 0)
        else:
            lax.fori_loop(0, nz, odd, 0)
            for dz in range(nz):
                dq_snd[dz] = (dqt[2 * dz + 1] * SCALE).astype(jnp.bfloat16)
                got_sib[dz] = remote(dq_snd.at[dz], dq_sib.at[dz], ctx_at(0, 0, 1), tp)
            lax.fori_loop(0, nz, even, 0)
        for i, dy in enumerate(order[2 * k:2 * k + 2]):
            if dy == 0:
                continue
            p = 2 * k + i
            part = acc[i * ROWS:(i + 1) * ROWS, :]
            dkv_snd[p, :, 0:HD] = (part[:, 0:HD] * SCALE).astype(jnp.bfloat16)
            dkv_snd[p, :, HD:2 * HD] = part[:, HD:2 * HD].astype(jnp.bfloat16)
            got_dkv[dy] = remote(dkv_snd.at[p], dkv_got.at[p], ctx_at(0, ny - dy, 0), tp)

    got_dq = {}
    for dz in far_first(nz):
        if dz:
            got_sib[dz].wait_recv()
            both = dqt[2 * dz] * SCALE + dq_sib[dz].astype(jnp.float32)
            dq_snd[nz + dz] = both.astype(jnp.bfloat16)
            got_dq[dz] = remote(dq_snd.at[nz + dz], dq_got.at[dz], ctx_at(nz - dz, 0, 0), tp)

    i = own % 2
    d_key = acc[i * ROWS:(i + 1) * ROWS, 0:HD] * SCALE
    d_value = acc[i * ROWS:(i + 1) * ROWS, HD:2 * HD]
    for dy in order:
        if dy:
            got_dkv[dy].wait_recv()
            d_key += dkv_got[place[dy], :, 0:HD].astype(jnp.float32)
            d_value += dkv_got[place[dy], :, HD:2 * HD].astype(jnp.float32)
    d_key = d_key * cosine - pltpu.roll(d_key, HD // 2, 1) * sine
    d_kv = jnp.concatenate([d_key, d_value], axis=1).astype(jnp.bfloat16)

    def term(dx, dl):
        rows = pl.ds(pl.multiple_of(tp_at(dx, dl) * WIDE, WIDE), WIDE)
        return matmul_nt(d_kv, wkv[rows, :]).astype(jnp.bfloat16)

    got_di = {}
    for dx in far_first(nx):
        for dl in reversed(range(nl)):
            if (dx, dl) != (0, 0):
                s = dx * nl + dl
                di_snd[s] = term(dx, dl)
                got_di[s] = remote(di_snd.at[s], di_got.at[s], ctx, tp_at(dx, dl))
    d_input = term(0, 0).astype(jnp.float32)

    got_sib[0].wait_recv()
    d_query = dqt[0] * SCALE + dq_sib[0].astype(jnp.float32)
    for dz in near_first(nz):
        got_dq[dz].wait_recv()
        d_query += dq_got[dz].astype(jnp.float32)
    for h in range(GROUP):
        cols = slice(h * HD, (h + 1) * HD)
        dq_res[:, cols] = d_query[:, cols].T.astype(jnp.bfloat16)
    store_dq = local(dq_res, dq_out)

    for s in got_di:
        got_di[s].wait_recv()
        d_input += di_got[s].astype(jnp.float32)
    di_res[...] = d_input.astype(jnp.bfloat16)
    store_di = local(di_res, di_out)
    for copy in sent:
        copy.wait_send()
    store_dq.wait()
    store_di.wait()


def body(grid, x_stash, w_key, w_value, query, out_stash, d_out, roster):
    nz, ny, nx, nl = grid
    nj, nt, chunks = 2 * nz, nx * nl, ny // 2
    bf16, f32 = jnp.bfloat16, jnp.float32
    half = ROPE_BASE ** (-(np.arange(HD // 2) * 2.0) / HD)
    freq = jnp.asarray(np.concatenate([half, half])[None, :].astype(np.float32))
    copies = (nt - 1) + 4 * (nj - 1) + 2 * (ny - 1) + nz + (nz - 1) + (nt - 1)
    vmem = pltpu.VMEM
    hbm = pl.BlockSpec(memory_space=pl.ANY)
    flops = 2 * nj * WIDE * ny * ROWS * HD * 5
    return pl.pallas_call(
        functools.partial(kernel, grid),
        out_shape=(
            jax.ShapeDtypeStruct((ROWS, WIDE), bf16),
            jax.ShapeDtypeStruct((ROWS, WIDE), bf16),
        ),
        in_specs=[hbm] * 6
        + [pl.BlockSpec(memory_space=pltpu.SMEM), pl.BlockSpec(memory_space=pltpu.VMEM)],
        out_specs=(hbm, hbm),
        scratch_shapes=[
            vmem((nt, ROWS, WIDE), bf16),
            vmem((nt * WIDE, 2 * HD), bf16),
            vmem((nj, ROWS, WIDE), bf16),
            vmem((nj, ROWS, WIDE), bf16),
            vmem((ROWS, WIDE), bf16),
            vmem((ny * ROWS, 2 * HD), bf16),
            vmem((chunks, HD, 2 * ROWS), bf16),
            vmem((ny * ROWS, HD), jnp.int32),
            vmem((nj, ROWS), jnp.int32),
            vmem((chunks, nj, 2 * ROWS, WIDE), f32),
            vmem((chunks, nj, 1, WIDE), f32),
            vmem((chunks, nj, 1, WIDE), f32),
            vmem((chunks, nj, 1, WIDE), f32),
            vmem((nj, 1, WIDE), f32),
            vmem((nj, nj, 1, WIDE), f32),
            vmem((nj, 1, WIDE), f32),
            vmem((nj, HD, WIDE), f32),
            vmem((2 * nz, HD, WIDE), bf16),
            vmem((nz, HD, WIDE), bf16),
            vmem((nz, HD, WIDE), bf16),
            vmem((2 * ROWS, 2 * HD), f32),
            vmem((ny, ROWS, 2 * HD), bf16),
            vmem((ny, ROWS, 2 * HD), bf16),
            vmem((nt, ROWS, WIDE), bf16),
            vmem((nt, ROWS, WIDE), bf16),
            vmem((ROWS, WIDE), bf16),
            vmem((ROWS, WIDE), bf16),
            pltpu.SemaphoreType.DMA((copies,)),
            pltpu.SemaphoreType.DMA((copies,)),
            pltpu.SemaphoreType.DMA((8,)),
        ],
        compiler_params=pltpu.CompilerParams(
            collective_id=0, has_side_effects=True, vmem_limit_bytes=56 * 1024 * 1024
        ),
        cost_estimate=pl.CostEstimate(
            flops=flops, bytes_accessed=4 * 1024 * 1024, transcendentals=nj * WIDE * ny * ROWS
        ),
    )(x_stash, w_key, w_value, query, out_stash, d_out, roster, freq)


def solution(mesh):
    grid = GRIDS[mesh.shape["ctx"], mesh.shape["tp"]]
    split = P("ctx", "tp")
    return jax.shard_map(
        functools.partial(body, grid),
        mesh=mesh,
        in_specs=(split, P(None, "tp"), P(None, "tp"), split, split, split, P()),
        out_specs=(split, split),
        check_vma=False,
    )
```

time: 1470 us -> 99.3 us (0.07); the launches traced: 1450 us -> 99.1 us
  waiting for transfers between devices: 522 us -> 0 us
  starting transfers between devices: 498 us -> 0 us
  local copies, waits for them, and re-layouts: 166 us -> 2.26 us
  matrix products: 131 us -> 0 us
  other arithmetic: 107 us -> 0 us
  Pallas kernels: 0 us -> 96.2 us
    ppermute x254 -> x0, starting transfers between devices: 497 us -> none  [shifted(): return lax.ppermute(value, axis, pairs)]
    ppermute x254 -> x0, waiting for transfers between devices: 356 us -> none  [shifted(): return lax.ppermute(value, axis, pairs)]
    gather x128 -> x0, local copies, waits for them, and re-layouts: 157 us -> none  [row_positions(): blocks = jnp.take(roster, row_ids // block_rows)]
    dot_general x388 -> x0, matrix products: 131 us -> none  [the longest x128 76.6 us: key_scores(): jnp.einsum('tkgd,skd->kgts', query_heads, key_heads, preferred_element_ty...]
    all_gather x2 -> x0, waiting for transfers between devices: 124 us -> none  [the longest x1 76.8 us: body(): received = lax.all_gather(own_keys, 'ctx', axis=0, tiled=True)]
    pallas_call x0 -> x1, Pallas kernels: none -> 96.2 us  [body(): pl.pallas_call(functools.partial(kernel, grid), out_shape=(jax.ShapeDtype...]
    add x192 -> x0, other arithmetic: 85.3 us -> none  [the longest x64 82.2 us: stats_block(): exp_total * jnp.exp(row_peak - new_peak) + jnp.sum(weights, axis=-1)]
    reduce_scatter x1 -> x0, waiting for transfers between devices: 40.5 us -> none  [body(): lax.psum_scatter(partial_sum.astype(jnp.bfloat16), 'tp', scatter_dimensio...]
  transfers between devices with their start and end apart: 257 -> 0, of which waited for: 188 -> 0; matrix products, arithmetic and copies ran while one was open for 10% -> 0% of each run, Pallas kernels for 0% -> 0%
where the time goes in v1:
time: 99.3 us; the launch traced here: 99.1 us
  Pallas kernels  96.2 us (97%)
  local copies, waits for them, and re-layouts  2.26 us (2%)
    pallas_call x1, Pallas kernels, body(): pl.pallas_call(functools.partial(kernel, grid), out_shape=(jax.ShapeDtype...  96.2 us
    unnamed x4, local copies, waits for them, and re-layouts  2.26 us

profile of v1, /device:TPU:1, one launch (start us, length us, event | category | flops | bytes accessed | tf_op | source)
XLA Modules:
  0.0 99.1 jit_solution(8052314059445871846)
XLA Ops:
  0.6 96.2 %shard_map.95 = (bf16[128,512]{1,0:T(8,128)(2,1)}, bf16[128,512]{1,0:T(8,128)(2,1)}) custom-call(bf16[128,512]{1,0:T(8,128)(2,1)} %x_in.1, bf16[4096,128]{1,0:T(8,128)(2,1)} %wk_in.1, bf16[4096,128]{1,0:T(8,128)(2,1)} %wv_in.1, bf16[128,512]{1,0:T(8,128)(2,1)} %q_in.1, bf16[128,512]{1,0:T(8,128)(2,1)} %o_in.1, bf16[128,512]{1,0:T(8,128)(2,1)} %g_in.1, ...), custom_call_target="tpu_custom_call" | custom-call | flops 5368709120 | bytes 4194304 | tf_op jit(solution)/shard_map/pallas_call | solution.py:358
  96.8 0.0 copy-start
  96.8 1.6 %copy.12 = bf16[128,512]{1,0:T(8,128)(2,1)} copy(bf16[128,512]{1,0:T(8,128)(2,1)} %get-tuple-element.4) | data formatting | bytes 262144
  98.4 0.0 copy-done
  98.4 0.7 copy.13
Async XLA Ops:
  96.8 1.6 %copy-start = (bf16[128,512]{1,0:T(8,128)(2,1)S(1)}, bf16[128,512]{1,0:T(8,128)(2,1)}, u32[]{:S(2)}) copy-start(bf16[128,512]{1,0:T(8,128)(2,1)} %get-tuple-element.5) | copy-start | bytes 393220

commit v2 on v1

v2 whole, which is shorter than its diff:
```python
import functools

import jax
import jax.numpy as jnp
import numpy as np
from jax import lax
from jax.experimental import pallas as pl
from jax.experimental.pallas import tpu as pltpu
from jax.sharding import PartitionSpec as P

HD = 128
GROUP = 4
BLOCK = 64
ROWS = 128
WIDE = GROUP * HD
ROPE_BASE = 500000.0
SCALE = HD ** -0.5
LOG2E = 1.4426950408889634
NEG = -1e30
FLOOR = -1e20

GRIDS = {(64, 8): (4, 8, 4, 2)}

NT = (((1,), (1,)), ((), ()))


def matmul_nt(a, b):
    return lax.dot_general(a, b, NT, preferred_element_type=jnp.float32)


def matmul(a, b):
    return jnp.dot(a, b, preferred_element_type=jnp.float32)


def stacked(block):
    return jnp.concatenate([block[:, h * HD:(h + 1) * HD] for h in range(GROUP)], axis=0)


def far_first(count):
    return sorted(range(count), key=lambda d: (-min(d, count - d), d))


def beside(count):
    return sorted({1 % count, count - 1} - {0})


def kernel(
    grid, x_in, wk_in, wv_in, q_in, o_in, g_in, roster, freq,
    dq_out, di_out,
    xg, wkv, qg, gg, ol, kv, kt, posk, posq, probs, peak, total, fac, lse_own, lse_got,
    delta, dqt, dq_snd, dq_sib, dq_half, dq_got, acc, dkv_snd, dkv_got, dkv_all, w_cols, dq_res, di_res,
    send_sem, recv_sem, local_sem,
):
    nz, ny, nx, nl = grid
    nj = 2 * nz
    chunks = ny // 2
    ctx, tp = lax.axis_index("ctx"), lax.axis_index("tp")
    z, y, c = ctx // (2 * ny), (ctx // 2) % ny, ctx % 2
    xi, zl = tp // nl, tp % nl

    def ctx_at(dz, dy, dc):
        return (((z + dz) % nz) * ny + (y + dy) % ny) * 2 + (c + dc) % 2

    def tp_at(dx, dl):
        return ((xi + dx) % nx) * nl + (zl + dl) % nl

    tp_peers = [(dx, dl) for dx in range(nx) for dl in range(nl) if (dx, dl) != (0, 0)]
    q_peers = [(dz, dc) for dz in range(nz) for dc in range(2) if (dz, dc) != (0, 0)]
    y_peers = list(range(1, ny))

    used = [0, 0]

    def local(src, dst):
        copy = pltpu.make_async_copy(src, dst, local_sem.at[used[0]])
        used[0] += 1
        copy.start()
        return copy

    sent = []

    def remote(src, dst, at_ctx, at_tp):
        i = used[1]
        used[1] += 1
        copy = pltpu.make_async_remote_copy(
            src_ref=src, dst_ref=dst, send_sem=send_sem.at[i], recv_sem=recv_sem.at[i],
            device_id=(at_ctx, at_tp), device_id_type=pl.DeviceIdType.MESH,
        )
        copy.start()
        sent.append(copy)
        return copy

    load_x = local(x_in, xg.at[0])
    load_wk = local(wk_in, wkv.at[:, 0:HD])
    load_wv = local(wv_in, wkv.at[:, HD:2 * HD])
    load_g = local(g_in, gg.at[0])
    load_o = local(o_in, ol)
    load_q = local(q_in, qg.at[0])

    barrier = pltpu.get_barrier_semaphore()
    partners = [(ctx, tp_at(dx, dl)) for dx, dl in tp_peers]
    partners += [(ctx_at(dz, 0, dc), tp) for dz, dc in q_peers]
    partners += [(ctx_at(0, dy, 0), tp) for dy in y_peers]
    for partner in partners:
        pl.semaphore_signal(barrier, inc=1, device_id=partner, device_id_type=pl.DeviceIdType.MESH)

    order = far_first(ny)
    place = {dy: p for p, dy in enumerate(order)}
    row_id = lax.broadcasted_iota(jnp.int32, (ROWS, HD), 0)
    lane_id = lax.broadcasted_iota(jnp.int32, (1, ROWS), 1)
    for p, dy in enumerate(order):
        at = ctx_at(0, ny - dy, 0)
        first, second = roster[2 * at] * BLOCK, roster[2 * at + 1] * BLOCK
        posk[p * ROWS:(p + 1) * ROWS, :] = row_id + jnp.where(row_id < BLOCK, first, second - BLOCK)
    for j in range(nj):
        at = ctx_at(nz - j // 2, 0, 2 - j % 2)
        first, second = roster[2 * at] * BLOCK, roster[2 * at + 1] * BLOCK
        posq[j:j + 1, :] = lane_id + jnp.where(lane_id < BLOCK, first, second - BLOCK)
    own = place[0]
    angle = posk[own * ROWS:(own + 1) * ROWS, :].astype(jnp.float32) * freq[...]
    cosine = jnp.cos(angle)
    lane = lax.broadcasted_iota(jnp.int32, (ROWS, HD), 1)
    sine = jnp.where(lane < HD // 2, -1.0, 1.0) * jnp.sin(angle)

    load_g.wait()
    load_o.wait()
    for h in range(GROUP):
        cols = slice(h * HD, (h + 1) * HD)
        product = gg[0, :, cols].astype(jnp.float32) * ol[:, cols].astype(jnp.float32)
        delta[0, :, cols] = jnp.sum(product.T, axis=0, keepdims=True)

    def project(dx, dl):
        at = ((xi + nx - dx) % nx) * nl + (zl + nl - dl) % nl
        rows = pl.ds(pl.multiple_of(at * WIDE, WIDE), WIDE)
        return matmul(xg[dx * nl + dl], wkv[rows, :])

    load_x.wait()
    load_wk.wait()
    load_wv.wait()
    raw = project(0, 0)

    pl.semaphore_wait(barrier, len(partners))

    low, high = slice(0, ROWS // 2), slice(ROWS // 2, ROWS)

    def tp_begin(src, buf):
        got = {}
        if nl > 1:
            got[0, 1] = remote(src, buf.at[1], ctx, tp_at(0, 1))
        for dx in beside(nx):
            got[dx, 0] = remote(src, buf.at[dx * nl], ctx, tp_at(dx, 0))
        return got

    def tp_partner(buf, got):
        if nl > 1:
            got[0, 1].wait_recv()
            for dx in beside(nx):
                got[dx, 1] = remote(buf.at[1], buf.at[dx * nl + 1], ctx, tp_at(dx, 0))

    def tp_sides(buf, got, dl):
        for dx in beside(nx):
            got[dx, dl].wait_recv()
            if nx == 4:
                part = low if dx == 1 else high
                got[2, dl, dx] = remote(
                    buf.at[dx * nl + dl, part, :], buf.at[2 * nl + dl, part, :], ctx, tp_at(dx, 0)
                )

    def tp_opposite(got, dl):
        for dx in beside(nx):
            got[2, dl, dx].wait_recv()

    def z_begin(src, buf):
        got = {}
        for dz in beside(nz):
            got[dz, 0] = remote(src, buf.at[2 * dz], ctx_at(dz, 0, 0), tp)
        got[0, 1] = remote(src, buf.at[1], ctx_at(0, 0, 1), tp)
        return got

    def z_sides(buf, got):
        for dz in beside(nz):
            got[dz, 0].wait_recv()
            if nz == 4:
                part = low if dz == 1 else high
                got[2, 0, dz] = remote(
                    buf.at[2 * dz, part, :], buf.at[4, part, :], ctx_at(dz, 0, 0), tp
                )
            got[dz, 1] = remote(buf.at[2 * dz], buf.at[2 * dz + 1], ctx_at(0, 0, 1), tp)

    def z_opposite(buf, got):
        if nz == 4:
            for dz in beside(nz):
                got[2, 0, dz].wait_recv()
            got[2, 1] = remote(buf.at[4], buf.at[5], ctx_at(0, 0, 1), tp)

    def z_finish(got):
        for dz in range(nz):
            got[dz, 1].wait_recv()

    got_x = tp_begin(x_in, xg)
    got_q = z_begin(q_in, qg)
    tp_partner(xg, got_x)
    tp_sides(xg, got_x, 0)
    if nl > 1:
        raw += project(0, 1)
    for dx in beside(nx):
        raw += project(dx, 0)
    z_sides(qg, got_q)
    got_g = z_begin(g_in, gg)
    got_delta = [
        remote(delta.at[0], delta.at[2 * dz + dc], ctx_at(dz, 0, dc), tp) for dz, dc in q_peers
    ]
    if nl > 1:
        tp_sides(xg, got_x, 1)
        for dx in beside(nx):
            raw += project(dx, 1)
    if nx == 4:
        for dl in range(nl):
            tp_opposite(got_x, dl)
            raw += project(2, dl)

    key_raw = raw[:, 0:HD]
    keys = key_raw * cosine + pltpu.roll(key_raw, HD // 2, 1) * sine
    own_rows = pl.ds(own * ROWS, ROWS)
    kv[own_rows, 0:HD] = keys.astype(jnp.bfloat16)
    kv[own_rows, HD:2 * HD] = raw[:, HD:2 * HD].astype(jnp.bfloat16)

    def kv_send(dy_from, dy_to, start=0, count=ROWS):
        src = kv.at[pl.ds(place[dy_from] * ROWS + start, count), :]
        dst = kv.at[pl.ds(place[dy_to] * ROWS + start, count), :]
        return remote(src, dst, ctx_at(0, (ny + dy_to - dy_from) % ny, 0), tp)

    got_kv = {}
    direct = [1, 7, 2, 6] if ny == 8 else y_peers
    for dy in direct:
        got_kv[dy] = [kv_send(0, dy)]
    z_opposite(qg, got_q)
    if ny == 8:
        got_kv[4] = []
        for dy, onward, start in ((2, 3, 0), (6, 5, ROWS // 2)):
            for copy in got_kv[dy]:
                copy.wait_recv()
            got_kv[dy] = []
            got_kv[onward] = [kv_send(dy, onward)]
            got_kv[4].append(kv_send(dy, 4, start, ROWS // 2))
    load_q.wait()
    z_finish(got_q)
    z_sides(gg, got_g)

    def slot_of(a):
        return ((z + nz - a // 2) % nz) * 2 + (c + 2 - a % 2) % 2

    def place_of(j):
        return ((z + nz - j // 2) % nz) * 2 + (c + 2 - j % 2) % 2

    def score_step(k, a):
        j = slot_of(a)
        rows = pl.ds(pl.multiple_of(k * 2 * ROWS, 2 * ROWS), 2 * ROWS)
        scores = matmul_nt(kv[rows, 0:HD], stacked(qg[j]))
        allowed = posk[rows, :] <= posq[pl.ds(j, 1), :]
        for h in range(GROUP):
            cols = slice(h * HD, (h + 1) * HD)
            part = jnp.where(allowed, scores[:, cols] * (SCALE * LOG2E), NEG)
            top = jnp.maximum(jnp.max(part, axis=0, keepdims=True), FLOOR)
            weight = jnp.exp2(part - top)
            probs[k, j, :, cols] = weight
            peak[k, a, :, cols] = top
            total[k, a, :, cols] = jnp.sum(weight, axis=0, keepdims=True)

    batch = nj // 2

    def send_totals(b):
        for i in range(batch):
            a = b * batch + i
            top = peak[0, a]
            for k in range(1, chunks):
                top = jnp.maximum(top, peak[k, a])
            mass = total[0, a] * jnp.exp2(peak[0, a] - top)
            for k in range(1, chunks):
                mass += total[k, a] * jnp.exp2(peak[k, a] - top)
            lse_own[b, i:i + 1, :] = jnp.where(
                mass > 0.0, top + jnp.log(jnp.maximum(mass, 1e-30)) * LOG2E, NEG
            )
        return [
            remote(lse_own.at[b], lse_got.at[2 * dz + dc, b], ctx_at(dz, 0, dc), tp)
            for dz, dc in q_peers
        ]

    def take_totals(b, got):
        for copy in got:
            copy.wait_recv()
        top = lse_own[b]
        for s in range(1, nj):
            top = jnp.maximum(top, lse_got[s, b])
        mass = jnp.exp2(lse_own[b] - top)
        for s in range(1, nj):
            mass += jnp.exp2(lse_got[s, b] - top)
        lse = top + jnp.log(mass) * LOG2E
        for k in range(chunks):
            for i in range(batch):
                fac[k, b * batch + i] = jnp.exp2(peak[k, b * batch + i] - lse[i:i + 1, :])

    def each(count, step):
        def run(i, carry):
            step(i)
            return carry

        lax.fori_loop(0, count, run, 0)

    for k in reversed(range(chunks)):
        for dy in order[2 * k:2 * k + 2]:
            for copy in got_kv.get(dy, []):
                copy.wait_recv()
        rows = slice(2 * k * ROWS, 2 * (k + 1) * ROWS)
        kt[k] = kv[rows, 0:HD].astype(jnp.float32).T.astype(jnp.bfloat16)
        each(batch, functools.partial(score_step, k))
    got_lse = [send_totals(0)]
    z_opposite(gg, got_g)

    mine = pl.ds(pl.multiple_of(c * HD, HD), HD)
    got_w = {}
    for dx, dl in tp_peers:
        rows = pl.ds(pl.multiple_of(tp_at(dx, dl) * WIDE, WIDE), WIDE)
        s = dx * nl + dl
        got_w[s] = remote(wkv.at[rows, mine], w_cols.at[s, :, mine], ctx, tp_at(dx, dl))

    each(batch * chunks, lambda i: score_step(i // batch, batch + i % batch))
    got_lse.append(send_totals(1))
    for copy in got_delta:
        copy.wait_recv()
    z_finish(got_g)
    take_totals(0, got_lse[0])

    got_dkv = {}
    got_sib = {}
    got_w_sib = {}
    for k in range(chunks):
        rows = slice(2 * k * ROWS, 2 * (k + 1) * ROWS)
        acc[...] = jnp.zeros_like(acc)

        def grad_step(j, k=k, rows=rows):
            gs, qs = stacked(gg[j]), stacked(qg[j])
            d_probs = matmul_nt(kv[rows, HD:2 * HD], gs)
            prob = probs[k, j] * fac[k, place_of(j)]
            d_scores = (prob * (d_probs - delta[j])).astype(jnp.bfloat16)
            acc[:, HD:2 * HD] += matmul(prob.astype(jnp.bfloat16), gs)
            acc[:, 0:HD] += matmul(d_scores, qs)
            part = matmul(kt[k], d_scores)
            if k == 0:
                dqt[j] = part
            else:
                dqt[j] += part

        if k == 0:
            each(batch, lambda a, step=grad_step: step(slot_of(a)))
            take_totals(1, got_lse[1])
            each(batch, lambda a, step=grad_step: step(slot_of(batch + a)))
        if 0 < k < chunks - 1:
            each(nj, grad_step)
        if k == max(chunks - 2, 0):
            for s in got_w:
                got_w[s].wait_recv()
                got_w_sib[s] = remote(
                    w_cols.at[s, :, mine], w_cols.at[s, :, mine], ctx_at(0, 0, 1), tp
                )
        if k == chunks - 1:
            if k:
                each(nz, lambda i, step=grad_step: step(2 * i + 1))
            for dz in far_first(nz):
                dq_snd[dz] = (dqt[2 * dz + 1] * SCALE).astype(jnp.bfloat16)
                got_sib[dz] = remote(dq_snd.at[dz], dq_sib.at[dz], ctx_at(0, 0, 1), tp)
            if k:
                each(nz, lambda i, step=grad_step: step(2 * i))
        for i, dy in enumerate(order[2 * k:2 * k + 2]):
            if dy == 0:
                continue
            p = 2 * k + i
            part = acc[i * ROWS:(i + 1) * ROWS, :]
            dkv_snd[p, :, 0:HD] = (part[:, 0:HD] * SCALE).astype(jnp.bfloat16)
            dkv_snd[p, :, HD:2 * HD] = part[:, HD:2 * HD].astype(jnp.bfloat16)
            got_dkv[dy] = remote(dkv_snd.at[p], dkv_got.at[p], ctx_at(0, ny - dy, 0), tp)

    def both_cores(dz):
        got_sib[dz].wait_recv()
        return dqt[2 * dz] * SCALE + dq_sib[dz].astype(jnp.float32)

    got_half = {}
    if nz == 4:
        dq_snd[6] = both_cores(2).astype(jnp.bfloat16)
        got_half[1] = remote(dq_snd.at[6, low, :], dq_half.at[low, :], ctx_at(3, 0, 0), tp)
        got_half[3] = remote(dq_snd.at[6, high, :], dq_half.at[high, :], ctx_at(1, 0, 0), tp)

    i = own % 2
    d_key = acc[i * ROWS:(i + 1) * ROWS, 0:HD] * SCALE
    d_value = acc[i * ROWS:(i + 1) * ROWS, HD:2 * HD]
    for dy in order:
        if dy:
            got_dkv[dy].wait_recv()
            d_key += dkv_got[place[dy], :, 0:HD].astype(jnp.float32)
            d_value += dkv_got[place[dy], :, HD:2 * HD].astype(jnp.float32)
    d_key = d_key * cosine - pltpu.roll(d_key, HD // 2, 1) * sine
    d_kv = jnp.concatenate([d_key, d_value], axis=1).astype(jnp.bfloat16)
    dkv_all[0] = d_kv
    got_all = tp_begin(dkv_all.at[0], dkv_all)

    got_dq = {}
    for dz in beside(nz):
        both = both_cores(dz)
        if nz == 4:
            got_half[dz].wait_recv()
            part = low if dz == 1 else high
            other = high if dz == 1 else low
            dq_snd[nz + dz, part, :] = (
                both[part] + dq_half[part, :].astype(jnp.float32)
            ).astype(jnp.bfloat16)
            dq_snd[nz + dz, other, :] = both[other].astype(jnp.bfloat16)
        else:
            dq_snd[nz + dz] = both.astype(jnp.bfloat16)
        got_dq[dz] = remote(dq_snd.at[nz + dz], dq_got.at[dz], ctx_at(nz - dz, 0, 0), tp)
    tp_partner(dkv_all, got_all)
    tp_sides(dkv_all, got_all, 0)

    def term(s, weights):
        return matmul_nt(dkv_all[s], weights).astype(jnp.bfloat16).astype(jnp.float32)

    for s in got_w_sib:
        got_w_sib[s].wait_recv()
    d_input = term(0, wkv[pl.ds(pl.multiple_of(tp * WIDE, WIDE), WIDE), :])
    if nl > 1:
        d_input += term(1, w_cols[1])
    for dx in beside(nx):
        d_input += term(dx * nl, w_cols[dx * nl])
    if nl > 1:
        tp_sides(dkv_all, got_all, 1)
        for dx in beside(nx):
            d_input += term(dx * nl + 1, w_cols[dx * nl + 1])
    if nx == 4:
        for dl in range(nl):
            tp_opposite(got_all, dl)
            d_input += term(2 * nl + dl, w_cols[2 * nl + dl])
    di_res[...] = d_input.astype(jnp.bfloat16)
    store_di = local(di_res, di_out)

    d_query = both_cores(0)
    for dz in beside(nz):
        got_dq[dz].wait_recv()
        d_query += dq_got[dz].astype(jnp.float32)
    for h in range(GROUP):
        cols = slice(h * HD, (h + 1) * HD)
        dq_res[:, cols] = d_query[:, cols].T.astype(jnp.bfloat16)
    store_dq = local(dq_res, dq_out)
    for copy in sent:
        copy.wait_send()
    store_dq.wait()
    store_di.wait()


def body(grid, x_stash, w_key, w_value, query, out_stash, d_out, roster):
    nz, ny, nx, nl = grid
    nj, nt, chunks = 2 * nz, nx * nl, ny // 2
    bf16, f32 = jnp.bfloat16, jnp.float32
    half = ROPE_BASE ** (-(np.arange(HD // 2) * 2.0) / HD)
    freq = jnp.asarray(np.concatenate([half, half])[None, :].astype(np.float32))
    copies = 128
    vmem = pltpu.VMEM
    hbm = pl.BlockSpec(memory_space=pl.ANY)
    flops = 2 * nj * WIDE * ny * ROWS * HD * 5
    return pl.pallas_call(
        functools.partial(kernel, grid),
        out_shape=(
            jax.ShapeDtypeStruct((ROWS, WIDE), bf16),
            jax.ShapeDtypeStruct((ROWS, WIDE), bf16),
        ),
        in_specs=[hbm] * 6
        + [pl.BlockSpec(memory_space=pltpu.SMEM), pl.BlockSpec(memory_space=pltpu.VMEM)],
        out_specs=(hbm, hbm),
        scratch_shapes=[
            vmem((nt, ROWS, WIDE), bf16),
            vmem((nt * WIDE, 2 * HD), bf16),
            vmem((nj, ROWS, WIDE), bf16),
            vmem((nj, ROWS, WIDE), bf16),
            vmem((ROWS, WIDE), bf16),
            vmem((ny * ROWS, 2 * HD), bf16),
            vmem((chunks, HD, 2 * ROWS), bf16),
            vmem((ny * ROWS, HD), jnp.int32),
            vmem((nj, ROWS), jnp.int32),
            vmem((chunks, nj, 2 * ROWS, WIDE), f32),
            vmem((chunks, nj, 1, WIDE), f32),
            vmem((chunks, nj, 1, WIDE), f32),
            vmem((chunks, nj, 1, WIDE), f32),
            vmem((2, nz, WIDE), f32),
            vmem((nj, 2, nz, WIDE), f32),
            vmem((nj, 1, WIDE), f32),
            vmem((nj, HD, WIDE), f32),
            vmem((2 * nz, HD, WIDE), bf16),
            vmem((nz, HD, WIDE), bf16),
            vmem((HD, WIDE), bf16),
            vmem((nz, HD, WIDE), bf16),
            vmem((2 * ROWS, 2 * HD), f32),
            vmem((ny, ROWS, 2 * HD), bf16),
            vmem((ny, ROWS, 2 * HD), bf16),
            vmem((nt, ROWS, 2 * HD), bf16),
            vmem((nt, WIDE, 2 * HD), bf16),
            vmem((ROWS, WIDE), bf16),
            vmem((ROWS, WIDE), bf16),
            pltpu.SemaphoreType.DMA((copies,)),
            pltpu.SemaphoreType.DMA((copies,)),
            pltpu.SemaphoreType.DMA((8,)),
        ],
        compiler_params=pltpu.CompilerParams(
            collective_id=0, has_side_effects=True, vmem_limit_bytes=56 * 1024 * 1024
        ),
        cost_estimate=pl.CostEstimate(
            flops=flops, bytes_accessed=4 * 1024 * 1024, transcendentals=nj * WIDE * ny * ROWS
        ),
    )(x_stash, w_key, w_value, query, out_stash, d_out, roster, freq)


def solution(mesh):
    grid = GRIDS[mesh.shape["ctx"], mesh.shape["tp"]]
    split = P("ctx", "tp")
    return jax.shard_map(
        functools.partial(body, grid),
        mesh=mesh,
        in_specs=(split, P(None, "tp"), P(None, "tp"), split, split, split, P()),
        out_specs=(split, split),
        check_vma=False,
    )
```

time: 99.3 us -> 94.6 us (0.953)
  the two profiles are of different devices: /device:TPU:1 before, /device:TPU:2 now
where the time goes in v2:
time: 94.6 us; the launch traced here: 94.5 us
  Pallas kernels  91.5 us (97%)
  local copies, waits for them, and re-layouts  2.26 us (2%)
    pallas_call x1, Pallas kernels, body(): pl.pallas_call(functools.partial(kernel, grid), out_shape=(jax.ShapeDtype...  91.5 us
    unnamed x4, local copies, waits for them, and re-layouts  2.26 us

profile of v2, /device:TPU:2, one launch (start us, length us, event | category | flops | bytes accessed | tf_op | source)
XLA Modules:
  0.0 94.5 jit_solution(16901435825084848241)
XLA Ops:
  0.6 91.5 %shard_map.95 = (bf16[128,512]{1,0:T(8,128)(2,1)}, bf16[128,512]{1,0:T(8,128)(2,1)}) custom-call(bf16[128,512]{1,0:T(8,128)(2,1)} %x_in.1, bf16[4096,128]{1,0:T(8,128)(2,1)} %wk_in.1, bf16[4096,128]{1,0:T(8,128)(2,1)} %wv_in.1, bf16[128,512]{1,0:T(8,128)(2,1)} %q_in.1, bf16[128,512]{1,0:T(8,128)(2,1)} %o_in.1, bf16[128,512]{1,0:T(8,128)(2,1)} %g_in.1, ...), custom_call_target="tpu_custom_call" | custom-call | flops 5368709120 | bytes 4194304 | tf_op jit(solution)/shard_map/pallas_call | solution.py:467
  92.2 0.0 copy-start
  92.2 1.6 %copy.12 = bf16[128,512]{1,0:T(8,128)(2,1)} copy(bf16[128,512]{1,0:T(8,128)(2,1)} %get-tuple-element.4) | data formatting | bytes 262144
  93.8 0.0 copy-done
  93.8 0.7 copy.13
Async XLA Ops:
  92.2 1.6 %copy-start = (bf16[128,512]{1,0:T(8,128)(2,1)S(1)}, bf16[128,512]{1,0:T(8,128)(2,1)}, u32[]{:S(2)}) copy-start(bf16[128,512]{1,0:T(8,128)(2,1)} %get-tuple-element.5) | copy-start | bytes 393220

commit v3 on v2

--- a/solution.py
+++ b/solution.py
@@ -40,6 +40,10 @@
     return sorted(range(count), key=lambda d: (-min(d, count - d), d))
 
 
+def key_order(ny):
+    return [4, 3, 5, 7, 2, 6, 1, 0] if ny == 8 else far_first(ny)
+
+
 def beside(count):
     return sorted({1 % count, count - 1} - {0})
 
@@ -48,7 +52,7 @@
     grid, x_in, wk_in, wv_in, q_in, o_in, g_in, roster, freq,
     dq_out, di_out,
     xg, wkv, qg, gg, ol, kv, kt, posk, posq, probs, peak, total, fac, lse_own, lse_got,
-    delta, dqt, dq_snd, dq_sib, dq_half, dq_got, acc, dkv_snd, dkv_got, dkv_all, w_cols, dq_res, di_res,
+    delta, dqt, dq_snd, dq_sib, dq_half, dq_got, acc, dkv_snd, dkv_relay, dkv_got, dkv_all, w_cols, dq_res, di_res,
     send_sem, recv_sem, local_sem,
 ):
     nz, ny, nx, nl = grid
@@ -103,7 +107,7 @@
     for partner in partners:
         pl.semaphore_signal(barrier, inc=1, device_id=partner, device_id_type=pl.DeviceIdType.MESH)
 
-    order = far_first(ny)
+    order = key_order(ny)
     place = {dy: p for p, dy in enumerate(order)}
     row_id = lax.broadcasted_iota(jnp.int32, (ROWS, HD), 0)
     lane_id = lax.broadcasted_iota(jnp.int32, (1, ROWS), 1)
@@ -142,12 +146,13 @@
 
     low, high = slice(0, ROWS // 2), slice(ROWS // 2, ROWS)
 
-    def tp_begin(src, buf):
+    def tp_begin(src, buf, across=False):
         got = {}
         if nl > 1:
             got[0, 1] = remote(src, buf.at[1], ctx, tp_at(0, 1))
-        for dx in beside(nx):
-            got[dx, 0] = remote(src, buf.at[dx * nl], ctx, tp_at(dx, 0))
+        for dl in range(nl if across else 1):
+            for dx in beside(nx):
+                got[dx, dl] = remote(src, buf.at[dx * nl + dl], ctx, tp_at(dx, dl))
         return got
 
     def tp_partner(buf, got):
@@ -197,20 +202,17 @@
             got[dz, 1].wait_recv()
 
     got_x = tp_begin(x_in, xg)
+    tp_partner(xg, got_x)
     got_q = z_begin(q_in, qg)
-    tp_partner(xg, got_x)
     tp_sides(xg, got_x, 0)
     if nl > 1:
         raw += project(0, 1)
     for dx in beside(nx):
         raw += project(dx, 0)
-    z_sides(qg, got_q)
-    got_g = z_begin(g_in, gg)
-    got_delta = [
-        remote(delta.at[0], delta.at[2 * dz + dc], ctx_at(dz, 0, dc), tp) for dz, dc in q_peers
-    ]
     if nl > 1:
         tp_sides(xg, got_x, 1)
+    z_sides(qg, got_q)
+    if nl > 1:
         for dx in beside(nx):
             raw += project(dx, 1)
     if nx == 4:
@@ -233,18 +235,22 @@
     direct = [1, 7, 2, 6] if ny == 8 else y_peers
     for dy in direct:
         got_kv[dy] = [kv_send(0, dy)]
+    got_g = z_begin(g_in, gg)
+    got_delta = [
+        remote(delta.at[0], delta.at[2 * dz + dc], ctx_at(dz, 0, dc), tp) for dz, dc in q_peers
+    ]
     z_opposite(qg, got_q)
-    if ny == 8:
-        got_kv[4] = []
-        for dy, onward, start in ((2, 3, 0), (6, 5, ROWS // 2)):
-            for copy in got_kv[dy]:
-                copy.wait_recv()
-            got_kv[dy] = []
-            got_kv[onward] = [kv_send(dy, onward)]
-            got_kv[4].append(kv_send(dy, 4, start, ROWS // 2))
     load_q.wait()
-    z_finish(got_q)
-    z_sides(gg, got_g)
+
+    def kv_forward():
+        if ny == 8:
+            got_kv[4] = []
+            for dy, onward, start in ((2, 3, 0), (6, 5, ROWS // 2)):
+                for copy in got_kv[dy]:
+                    copy.wait_recv()
+                got_kv[dy] = []
+                got_kv[onward] = [kv_send(dy, onward)]
+                got_kv[4].append(kv_send(dy, 4, start, ROWS // 2))
 
     def slot_of(a):
         return ((z + nz - a // 2) % nz) * 2 + (c + 2 - a % 2) % 2
@@ -300,31 +306,53 @@
                 fac[k, b * batch + i] = jnp.exp2(peak[k, b * batch + i] - lse[i:i + 1, :])
 
     def each(count, step):
+        unit = 4 if count % 4 == 0 else 1
+
         def run(i, carry):
-            step(i)
+            for u in range(unit):
+                step(i * unit + u)
             return carry
 
-        lax.fori_loop(0, count, run, 0)
-
+        lax.fori_loop(0, count // unit, run, 0)
+
+    mine = pl.ds(pl.multiple_of(c * HD, HD), HD)
+    got_w = {}
+
+    def send_weights(peers):
+        for dx, dl in peers:
+            rows = pl.ds(pl.multiple_of(tp_at(dx, dl) * WIDE, WIDE), WIDE)
+            s = dx * nl + dl
+            got_w[s] = remote(wkv.at[rows, mine], w_cols.at[s, :, mine], ctx, tp_at(dx, dl))
+
+    got_w_sib = {}
+
+    def share_weights(slots):
+        for s in slots:
+            if s not in got_w_sib:
+                got_w[s].wait_recv()
+                got_w_sib[s] = remote(
+                    w_cols.at[s, :, mine], w_cols.at[s, :, mine], ctx_at(0, 0, 1), tp
+                )
+
+    z_finish(got_q)
     for k in reversed(range(chunks)):
         for dy in order[2 * k:2 * k + 2]:
             for copy in got_kv.get(dy, []):
                 copy.wait_recv()
         rows = slice(2 * k * ROWS, 2 * (k + 1) * ROWS)
         kt[k] = kv[rows, 0:HD].astype(jnp.float32).T.astype(jnp.bfloat16)
-        each(batch, functools.partial(score_step, k))
-    got_lse = [send_totals(0)]
+        if k:
+            each(nj, functools.partial(score_step, k))
+        if k == chunks - 1:
+            kv_forward()
+            send_weights([(dx, dl) for dx, dl in tp_peers if dl == 0])
+        if k == max(chunks - 2, 0):
+            z_sides(gg, got_g)
+    got_lse = []
+    for b in range(2):
+        each(batch, lambda i, first=b * batch: score_step(0, first + i))
+        got_lse.append(send_totals(b))
     z_opposite(gg, got_g)
-
-    mine = pl.ds(pl.multiple_of(c * HD, HD), HD)
-    got_w = {}
-    for dx, dl in tp_peers:
-        rows = pl.ds(pl.multiple_of(tp_at(dx, dl) * WIDE, WIDE), WIDE)
-        s = dx * nl + dl
-        got_w[s] = remote(wkv.at[rows, mine], w_cols.at[s, :, mine], ctx, tp_at(dx, dl))
-
-    each(batch * chunks, lambda i: score_step(i // batch, batch + i % batch))
-    got_lse.append(send_totals(1))
     for copy in got_delta:
         copy.wait_recv()
     z_finish(got_g)
@@ -332,7 +360,12 @@
 
     got_dkv = {}
     got_sib = {}
-    got_w_sib = {}
+    got_relay = {}
+
+    def dkv_send(dy, to, dst, start=0, count=ROWS):
+        src = dkv_snd.at[place[dy], pl.ds(start, count), :]
+        return remote(src, dst.at[pl.ds(start, count), :], ctx_at(0, (ny + to) % ny, 0), tp)
+
     for k in range(chunks):
         rows = slice(2 * k * ROWS, 2 * (k + 1) * ROWS)
         acc[...] = jnp.zeros_like(acc)
@@ -353,15 +386,10 @@
         if k == 0:
             each(batch, lambda a, step=grad_step: step(slot_of(a)))
             take_totals(1, got_lse[1])
+            send_weights([(dx, dl) for dx, dl in tp_peers if dl])
             each(batch, lambda a, step=grad_step: step(slot_of(batch + a)))
         if 0 < k < chunks - 1:
             each(nj, grad_step)
-        if k == max(chunks - 2, 0):
-            for s in got_w:
-                got_w[s].wait_recv()
-                got_w_sib[s] = remote(
-                    w_cols.at[s, :, mine], w_cols.at[s, :, mine], ctx_at(0, 0, 1), tp
-                )
         if k == chunks - 1:
             if k:
                 each(nz, lambda i, step=grad_step: step(2 * i + 1))
@@ -375,9 +403,30 @@
                 continue
             p = 2 * k + i
             part = acc[i * ROWS:(i + 1) * ROWS, :]
-            dkv_snd[p, :, 0:HD] = (part[:, 0:HD] * SCALE).astype(jnp.bfloat16)
-            dkv_snd[p, :, HD:2 * HD] = part[:, HD:2 * HD].astype(jnp.bfloat16)
-            got_dkv[dy] = remote(dkv_snd.at[p], dkv_got.at[p], ctx_at(0, ny - dy, 0), tp)
+            d_key, d_value = part[:, 0:HD] * SCALE, part[:, HD:2 * HD]
+            if ny == 8 and dy in (2, 6):
+                side, half = (0, low) if dy == 2 else (1, high)
+                got_relay[dy].wait_recv()
+                got_relay[4, dy].wait_recv()
+                d_key += dkv_relay[side, :, 0:HD].astype(jnp.float32)
+                d_value += dkv_relay[side, :, HD:2 * HD].astype(jnp.float32)
+                more = dkv_relay[2, half, :].astype(jnp.float32)
+                none = jnp.zeros_like(more)
+                more = jnp.concatenate([more, none] if dy == 2 else [none, more], axis=0)
+                d_key += more[:, 0:HD]
+                d_value += more[:, HD:2 * HD]
+            dkv_snd[p, :, 0:HD] = d_key.astype(jnp.bfloat16)
+            dkv_snd[p, :, HD:2 * HD] = d_value.astype(jnp.bfloat16)
+            if ny == 8 and dy == 4:
+                got_relay[4, 2] = dkv_send(4, -2, dkv_relay.at[2], 0, ROWS // 2)
+                got_relay[4, 6] = dkv_send(4, 2, dkv_relay.at[2], ROWS // 2, ROWS // 2)
+            elif ny == 8 and dy in (3, 5):
+                side = 0 if dy == 3 else 1
+                got_relay[2 if dy == 3 else 6] = dkv_send(dy, -1 if dy == 3 else 1, dkv_relay.at[side])
+            else:
+                got_dkv[dy] = dkv_send(dy, -dy, dkv_got.at[p])
+        if k == min(1, chunks - 1):
+            share_weights([dx * nl for dx, dl in tp_peers if dl == 0])
 
     def both_cores(dz):
         got_sib[dz].wait_recv()
@@ -385,22 +434,22 @@
 
     got_half = {}
     if nz == 4:
-        dq_snd[6] = both_cores(2).astype(jnp.bfloat16)
-        got_half[1] = remote(dq_snd.at[6, low, :], dq_half.at[low, :], ctx_at(3, 0, 0), tp)
-        got_half[3] = remote(dq_snd.at[6, high, :], dq_half.at[high, :], ctx_at(1, 0, 0), tp)
+        dq_snd[2 * nz - 2] = both_cores(2).astype(jnp.bfloat16)
+        got_half[1] = remote(dq_snd.at[2 * nz - 2, low, :], dq_half.at[low, :], ctx_at(3, 0, 0), tp)
+        got_half[3] = remote(dq_snd.at[2 * nz - 2, high, :], dq_half.at[high, :], ctx_at(1, 0, 0), tp)
 
     i = own % 2
     d_key = acc[i * ROWS:(i + 1) * ROWS, 0:HD] * SCALE
     d_value = acc[i * ROWS:(i + 1) * ROWS, HD:2 * HD]
-    for dy in order:
-        if dy:
-            got_dkv[dy].wait_recv()
-            d_key += dkv_got[place[dy], :, 0:HD].astype(jnp.float32)
-            d_value += dkv_got[place[dy], :, HD:2 * HD].astype(jnp.float32)
+    for dy in got_dkv:
+        got_dkv[dy].wait_recv()
+        d_key += dkv_got[place[dy], :, 0:HD].astype(jnp.float32)
+        d_value += dkv_got[place[dy], :, HD:2 * HD].astype(jnp.float32)
     d_key = d_key * cosine - pltpu.roll(d_key, HD // 2, 1) * sine
     d_kv = jnp.concatenate([d_key, d_value], axis=1).astype(jnp.bfloat16)
     dkv_all[0] = d_kv
-    got_all = tp_begin(dkv_all.at[0], dkv_all)
+    got_all = tp_begin(dkv_all.at[0], dkv_all, across=True)
+    share_weights([dx * nl + dl for dx, dl in tp_peers if dl])
 
     got_dq = {}
     for dz in beside(nz):
@@ -416,8 +465,10 @@
         else:
             dq_snd[nz + dz] = both.astype(jnp.bfloat16)
         got_dq[dz] = remote(dq_snd.at[nz + dz], dq_got.at[dz], ctx_at(nz - dz, 0, 0), tp)
-    tp_partner(dkv_all, got_all)
-    tp_sides(dkv_all, got_all, 0)
+    for dl in range(nl):
+        tp_sides(dkv_all, got_all, dl)
+    if nl > 1:
+        got_all[0, 1].wait_recv()
 
     def term(s, weights):
         return matmul_nt(dkv_all[s], weights).astype(jnp.bfloat16).astype(jnp.float32)
@@ -430,7 +481,6 @@
     for dx in beside(nx):
         d_input += term(dx * nl, w_cols[dx * nl])
     if nl > 1:
-        tp_sides(dkv_all, got_all, 1)
         for dx in beside(nx):
             d_input += term(dx * nl + 1, w_cols[dx * nl + 1])
     if nx == 4:
@@ -497,6 +547,7 @@
             vmem((nz, HD, WIDE), bf16),
             vmem((2 * ROWS, 2 * HD), f32),
             vmem((ny, ROWS, 2 * HD), bf16),
+            vmem((3, ROWS, 2 * HD), bf16),
             vmem((ny, ROWS, 2 * HD), bf16),
             vmem((nt, ROWS, 2 * HD), bf16),
             vmem((nt, WIDE, 2 * HD), bf16),

time: 94.6 us -> 83.8 us (0.89)
  the two profiles are of different devices: /device:TPU:2 before, /device:TPU:1 now
where the time goes in v3:
time: 83.8 us; the launch traced here: 82.5 us
  Pallas kernels  79.6 us (95%)
  local copies, waits for them, and re-layouts  2.26 us (3%)
    pallas_call x1, Pallas kernels, body(): pl.pallas_call(functools.partial(kernel, grid), out_shape=(jax.ShapeDtype...  79.6 us
    unnamed x4, local copies, waits for them, and re-layouts  2.26 us

profile of v3, /device:TPU:1, one launch (start us, length us, event | category | flops | bytes accessed | tf_op | source)
XLA Modules:
  0.0 82.5 jit_solution(6624294997152768116)
XLA Ops:
  0.6 79.6 %shard_map.95 = (bf16[128,512]{1,0:T(8,128)(2,1)}, bf16[128,512]{1,0:T(8,128)(2,1)}) custom-call(bf16[128,512]{1,0:T(8,128)(2,1)} %x_in.1, bf16[4096,128]{1,0:T(8,128)(2,1)} %wk_in.1, bf16[4096,128]{1,0:T(8,128)(2,1)} %wv_in.1, bf16[128,512]{1,0:T(8,128)(2,1)} %q_in.1, bf16[128,512]{1,0:T(8,128)(2,1)} %o_in.1, bf16[128,512]{1,0:T(8,128)(2,1)} %g_in.1, ...), custom_call_target="tpu_custom_call" | custom-call | flops 5368709120 | bytes 4194304 | tf_op jit(solution)/shard_map/pallas_call | solution.py:517
  80.3 0.0 copy-start
  80.3 1.6 %copy.12 = bf16[128,512]{1,0:T(8,128)(2,1)} copy(bf16[128,512]{1,0:T(8,128)(2,1)} %get-tuple-element.4) | data formatting | bytes 262144
  81.9 0.0 copy-done
  81.9 0.7 copy.13
Async XLA Ops:
  80.3 1.6 %copy-start = (bf16[128,512]{1,0:T(8,128)(2,1)S(1)}, bf16[128,512]{1,0:T(8,128)(2,1)}, u32[]{:S(2)}) copy-start(bf16[128,512]{1,0:T(8,128)(2,1)} %get-tuple-element.5) | copy-start | bytes 393220

commit v4 on v3

--- a/solution.py
+++ b/solution.py
@@ -52,7 +52,7 @@
     grid, x_in, wk_in, wv_in, q_in, o_in, g_in, roster, freq,
     dq_out, di_out,
     xg, wkv, qg, gg, ol, kv, kt, posk, posq, probs, peak, total, fac, lse_own, lse_got,
-    delta, dqt, dq_snd, dq_sib, dq_half, dq_got, acc, dkv_snd, dkv_relay, dkv_got, dkv_all, w_cols, dq_res, di_res,
+    delta, ahead, dqt, dq_snd, dq_sib, dq_half, dq_got, acc, dkv_snd, dkv_relay, dkv_got, dkv_all, w_cols, di_snd, di_got, dq_res, di_res,
     send_sem, recv_sem, local_sem,
 ):
     nz, ny, nx, nl = grid
@@ -68,9 +68,9 @@
     def tp_at(dx, dl):
         return ((xi + dx) % nx) * nl + (zl + dl) % nl
 
-    tp_peers = [(dx, dl) for dx in range(nx) for dl in range(nl) if (dx, dl) != (0, 0)]
+    tp_peers = [(dx, 0) for dx in range(1, nx)] + [(0, dl) for dl in range(1, nl)]
     q_peers = [(dz, dc) for dz in range(nz) for dc in range(2) if (dz, dc) != (0, 0)]
-    y_peers = list(range(1, ny))
+    direct = [1, 7, 2, 6] if ny == 8 else list(range(1, ny))
 
     used = [0, 0]
 
@@ -103,9 +103,90 @@
     barrier = pltpu.get_barrier_semaphore()
     partners = [(ctx, tp_at(dx, dl)) for dx, dl in tp_peers]
     partners += [(ctx_at(dz, 0, dc), tp) for dz, dc in q_peers]
-    partners += [(ctx_at(0, dy, 0), tp) for dy in y_peers]
+    partners += [(ctx_at(0, dy, 0), tp) for dy in direct]
     for partner in partners:
         pl.semaphore_signal(barrier, inc=1, device_id=partner, device_id_type=pl.DeviceIdType.MESH)
+
+    pl.semaphore_wait(barrier, len(partners))
+
+    low, high = slice(0, ROWS // 2), slice(ROWS // 2, ROWS)
+
+    def halves(step):
+        return (low, high) if step == 1 else (high, low)
+
+    def tp_round(src, buf, dl):
+        got = {}
+        for turn in range(2):
+            for dx in beside(nx):
+                part = halves(dx)[turn]
+                got[dx, dl, turn] = remote(
+                    src.at[part, :], buf.at[dx * nl + dl, part, :], ctx, tp_at(dx, 0)
+                )
+        return got
+
+    def tp_begin(src, buf):
+        got = {}
+        if nl > 1:
+            got[0, 1] = remote(src, buf.at[1], ctx, tp_at(0, 1))
+        got.update(tp_round(src, buf, 0))
+        return got
+
+    def tp_partner(buf, got):
+        if nl > 1:
+            got[0, 1].wait_recv()
+            got.update(tp_round(buf.at[1], buf, 1))
+
+    def tp_sides(buf, got, dl):
+        for dx in beside(nx):
+            got[dx, dl, 0].wait_recv()
+            if nx == 4:
+                part = halves(dx)[0]
+                got[2, dl, dx] = remote(
+                    buf.at[dx * nl + dl, part, :], buf.at[2 * nl + dl, part, :], ctx, tp_at(dx, 0)
+                )
+        for dx in beside(nx):
+            got[dx, dl, 1].wait_recv()
+
+    def tp_opposite(got, dl):
+        for dx in beside(nx):
+            got[2, dl, dx].wait_recv()
+
+    def z_begin(src, buf):
+        got = {}
+        for turn in range(2):
+            for dz in beside(nz):
+                part = halves(dz)[turn]
+                got[dz, 0, turn] = remote(
+                    src.at[part, :], buf.at[2 * dz, part, :], ctx_at(dz, 0, 0), tp
+                )
+        got[0, 1] = remote(src, buf.at[1], ctx_at(0, 0, 1), tp)
+        return got
+
+    def z_sides(buf, got):
+        for dz in beside(nz):
+            got[dz, 0, 0].wait_recv()
+            if nz == 4:
+                part = halves(dz)[0]
+                got[2, 0, dz] = remote(
+                    buf.at[2 * dz, part, :], buf.at[4, part, :], ctx_at(dz, 0, 0), tp
+                )
+
+    def z_rest(buf, got):
+        for dz in beside(nz):
+            got[dz, 0, 1].wait_recv()
+            got[dz, 1] = remote(buf.at[2 * dz], buf.at[2 * dz + 1], ctx_at(0, 0, 1), tp)
+
+    def z_opposite(buf, got):
+        if nz == 4:
+            for dz in beside(nz):
+                got[2, 0, dz].wait_recv()
+            got[2, 1] = remote(buf.at[4], buf.at[5], ctx_at(0, 0, 1), tp)
+
+    def z_finish(got):
+        for dz in range(nz):
+            got[dz, 1].wait_recv()
+
+    got_x = tp_begin(x_in, xg)
 
     order = key_order(ny)
     place = {dy: p for p, dy in enumerate(order)}
@@ -142,66 +223,6 @@
     load_wv.wait()
     raw = project(0, 0)
 
-    pl.semaphore_wait(barrier, len(partners))
-
-    low, high = slice(0, ROWS // 2), slice(ROWS // 2, ROWS)
-
-    def tp_begin(src, buf, across=False):
-        got = {}
-        if nl > 1:
-            got[0, 1] = remote(src, buf.at[1], ctx, tp_at(0, 1))
-        for dl in range(nl if across else 1):
-            for dx in beside(nx):
-                got[dx, dl] = remote(src, buf.at[dx * nl + dl], ctx, tp_at(dx, dl))
-        return got
-
-    def tp_partner(buf, got):
-        if nl > 1:
-            got[0, 1].wait_recv()
-            for dx in beside(nx):
-                got[dx, 1] = remote(buf.at[1], buf.at[dx * nl + 1], ctx, tp_at(dx, 0))
-
-    def tp_sides(buf, got, dl):
-        for dx in beside(nx):
-            got[dx, dl].wait_recv()
-            if nx == 4:
-                part = low if dx == 1 else high
-                got[2, dl, dx] = remote(
-                    buf.at[dx * nl + dl, part, :], buf.at[2 * nl + dl, part, :], ctx, tp_at(dx, 0)
-                )
-
-    def tp_opposite(got, dl):
-        for dx in beside(nx):
-            got[2, dl, dx].wait_recv()
-
-    def z_begin(src, buf):
-        got = {}
-        for dz in beside(nz):
-            got[dz, 0] = remote(src, buf.at[2 * dz], ctx_at(dz, 0, 0), tp)
-        got[0, 1] = remote(src, buf.at[1], ctx_at(0, 0, 1), tp)
-        return got
-
-    def z_sides(buf, got):
-        for dz in beside(nz):
-            got[dz, 0].wait_recv()
-            if nz == 4:
-                part = low if dz == 1 else high
-                got[2, 0, dz] = remote(
-                    buf.at[2 * dz, part, :], buf.at[4, part, :], ctx_at(dz, 0, 0), tp
-                )
-            got[dz, 1] = remote(buf.at[2 * dz], buf.at[2 * dz + 1], ctx_at(0, 0, 1), tp)
-
-    def z_opposite(buf, got):
-        if nz == 4:
-            for dz in beside(nz):
-                got[2, 0, dz].wait_recv()
-            got[2, 1] = remote(buf.at[4], buf.at[5], ctx_at(0, 0, 1), tp)
-
-    def z_finish(got):
-        for dz in range(nz):
-            got[dz, 1].wait_recv()
-
-    got_x = tp_begin(x_in, xg)
     tp_partner(xg, got_x)
     got_q = z_begin(q_in, qg)
     tp_sides(xg, got_x, 0)
@@ -232,14 +253,13 @@
         return remote(src, dst, ctx_at(0, (ny + dy_to - dy_from) % ny, 0), tp)
 
     got_kv = {}
-    direct = [1, 7, 2, 6] if ny == 8 else y_peers
     for dy in direct:
         got_kv[dy] = [kv_send(0, dy)]
+    z_rest(qg, got_q)
     got_g = z_begin(g_in, gg)
     got_delta = [
         remote(delta.at[0], delta.at[2 * dz + dc], ctx_at(dz, 0, dc), tp) for dz, dc in q_peers
     ]
-    z_opposite(qg, got_q)
     load_q.wait()
 
     def kv_forward():
@@ -318,48 +338,89 @@
     mine = pl.ds(pl.multiple_of(c * HD, HD), HD)
     got_w = {}
 
-    def send_weights(peers):
-        for dx, dl in peers:
+    def send_weights():
+        for dx, dl in [(dx, dl) for dl in reversed(range(nl)) for dx in range(1, nx)]:
             rows = pl.ds(pl.multiple_of(tp_at(dx, dl) * WIDE, WIDE), WIDE)
             s = dx * nl + dl
-            got_w[s] = remote(wkv.at[rows, mine], w_cols.at[s, :, mine], ctx, tp_at(dx, dl))
+            got_w[s] = remote(wkv.at[rows, mine], w_cols.at[s, :, mine], ctx, tp_at(dx, 0))
 
     got_w_sib = {}
 
-    def share_weights(slots):
-        for s in slots:
-            if s not in got_w_sib:
-                got_w[s].wait_recv()
-                got_w_sib[s] = remote(
-                    w_cols.at[s, :, mine], w_cols.at[s, :, mine], ctx_at(0, 0, 1), tp
-                )
-
-    z_finish(got_q)
-    for k in reversed(range(chunks)):
+    def share_weights():
+        for s in got_w:
+            got_w[s].wait_recv()
+            got_w_sib[s] = remote(
+                w_cols.at[s, :, mine], w_cols.at[s, :, mine], ctx_at(0, 0, 1), tp
+            )
+
+    def take_keys(k):
         for dy in order[2 * k:2 * k + 2]:
             for copy in got_kv.get(dy, []):
                 copy.wait_recv()
-        rows = slice(2 * k * ROWS, 2 * (k + 1) * ROWS)
-        kt[k] = kv[rows, 0:HD].astype(jnp.float32).T.astype(jnp.bfloat16)
-        if k:
-            each(nj, functools.partial(score_step, k))
+
+    def scores_of(k, slots):
+        for j in slots:
+            score_step(k, place_of(j))
+
+    late = [4, 5] if nz == 4 else []
+    early = [j for j in range(nj) if j not in late]
+    z_opposite(qg, got_q)
+    got_q[0, 1].wait_recv()
+    for dz in beside(nz):
+        got_q[dz, 1].wait_recv()
+    ahead_of_rest = [k for k in (chunks - 1, chunks - 2) if k > 0]
+    if not ahead_of_rest:
+        kv_forward()
+    for k in ahead_of_rest:
+        take_keys(k)
+        scores_of(k, early)
         if k == chunks - 1:
             kv_forward()
-            send_weights([(dx, dl) for dx, dl in tp_peers if dl == 0])
-        if k == max(chunks - 2, 0):
-            z_sides(gg, got_g)
+            send_weights()
+    z_sides(gg, got_g)
+    if late:
+        got_q[2, 1].wait_recv()
+        for k in ahead_of_rest:
+            scores_of(k, late)
+    z_rest(gg, got_g)
+    for k in reversed(range(1, max(chunks - 2, 1))):
+        take_keys(k)
+        each(nj, functools.partial(score_step, k))
+    take_keys(0)
+    if not ahead_of_rest:
+        send_weights()
     got_lse = []
     for b in range(2):
         each(batch, lambda i, first=b * batch: score_step(0, first + i))
         got_lse.append(send_totals(b))
     z_opposite(gg, got_g)
+    for k in range(chunks):
+        rows = slice(2 * k * ROWS, 2 * (k + 1) * ROWS)
+        kt[k] = kv[rows, 0:HD].astype(jnp.float32).T.astype(jnp.bfloat16)
     for copy in got_delta:
         copy.wait_recv()
     z_finish(got_g)
+
+    def first_d_probs(j):
+        ahead[j] = matmul_nt(kv[0:2 * ROWS, HD:2 * HD], stacked(gg[j])) - delta[j]
+
+    each(nj, first_d_probs)
     take_totals(0, got_lse[0])
 
     got_dkv = {}
     got_sib = {}
+    def both_cores(dz):
+        got_sib[dz].wait_recv()
+        return dqt[2 * dz] * SCALE + dq_sib[dz].astype(jnp.float32)
+
+    got_half = {}
+    def send_halves():
+        if nz != 4:
+            return
+        dq_snd[2 * nz - 2] = both_cores(2).astype(jnp.bfloat16)
+        got_half[1] = remote(dq_snd.at[2 * nz - 2, low, :], dq_half.at[low, :], ctx_at(3, 0, 0), tp)
+        got_half[3] = remote(dq_snd.at[2 * nz - 2, high, :], dq_half.at[high, :], ctx_at(1, 0, 0), tp)
+
     got_relay = {}
 
     def dkv_send(dy, to, dst, start=0, count=ROWS):
@@ -372,9 +433,12 @@
 
         def grad_step(j, k=k, rows=rows):
             gs, qs = stacked(gg[j]), stacked(qg[j])
-            d_probs = matmul_nt(kv[rows, HD:2 * HD], gs)
+            if k == 0:
+                d_probs = ahead[j]
+            else:
+                d_probs = matmul_nt(kv[rows, HD:2 * HD], gs) - delta[j]
             prob = probs[k, j] * fac[k, place_of(j)]
-            d_scores = (prob * (d_probs - delta[j])).astype(jnp.bfloat16)
+            d_scores = (prob * d_probs).astype(jnp.bfloat16)
             acc[:, HD:2 * HD] += matmul(prob.astype(jnp.bfloat16), gs)
             acc[:, 0:HD] += matmul(d_scores, qs)
             part = matmul(kt[k], d_scores)
@@ -386,7 +450,6 @@
         if k == 0:
             each(batch, lambda a, step=grad_step: step(slot_of(a)))
             take_totals(1, got_lse[1])
-            send_weights([(dx, dl) for dx, dl in tp_peers if dl])
             each(batch, lambda a, step=grad_step: step(slot_of(batch + a)))
         if 0 < k < chunks - 1:
             each(nj, grad_step)
@@ -397,7 +460,13 @@
                 dq_snd[dz] = (dqt[2 * dz + 1] * SCALE).astype(jnp.bfloat16)
                 got_sib[dz] = remote(dq_snd.at[dz], dq_sib.at[dz], ctx_at(0, 0, 1), tp)
             if k:
-                each(nz, lambda i, step=grad_step: step(2 * i))
+                for dz in [dz for dz in (2, 1) if dz < nz]:
+                    grad_step(2 * dz)
+                send_halves()
+                for dz in [dz for dz in (3, 0) if dz < nz]:
+                    grad_step(2 * dz)
+            else:
+                send_halves()
         for i, dy in enumerate(order[2 * k:2 * k + 2]):
             if dy == 0:
                 continue
@@ -425,18 +494,8 @@
                 got_relay[2 if dy == 3 else 6] = dkv_send(dy, -1 if dy == 3 else 1, dkv_relay.at[side])
             else:
                 got_dkv[dy] = dkv_send(dy, -dy, dkv_got.at[p])
-        if k == min(1, chunks - 1):
-            share_weights([dx * nl for dx, dl in tp_peers if dl == 0])
-
-    def both_cores(dz):
-        got_sib[dz].wait_recv()
-        return dqt[2 * dz] * SCALE + dq_sib[dz].astype(jnp.float32)
-
-    got_half = {}
-    if nz == 4:
-        dq_snd[2 * nz - 2] = both_cores(2).astype(jnp.bfloat16)
-        got_half[1] = remote(dq_snd.at[2 * nz - 2, low, :], dq_half.at[low, :], ctx_at(3, 0, 0), tp)
-        got_half[3] = remote(dq_snd.at[2 * nz - 2, high, :], dq_half.at[high, :], ctx_at(1, 0, 0), tp)
+        if k == max(chunks - 2, 0):
+            share_weights()
 
     i = own % 2
     d_key = acc[i * ROWS:(i + 1) * ROWS, 0:HD] * SCALE
@@ -448,8 +507,7 @@
     d_key = d_key * cosine - pltpu.roll(d_key, HD // 2, 1) * sine
     d_kv = jnp.concatenate([d_key, d_value], axis=1).astype(jnp.bfloat16)
     dkv_all[0] = d_kv
-    got_all = tp_begin(dkv_all.at[0], dkv_all, across=True)
-    share_weights([dx * nl + dl for dx, dl in tp_peers if dl])
+    got_all = tp_round(dkv_all.at[0], dkv_all, 0)
 
     got_dq = {}
     for dz in beside(nz):
@@ -465,30 +523,30 @@
         else:
             dq_snd[nz + dz] = both.astype(jnp.bfloat16)
         got_dq[dz] = remote(dq_snd.at[nz + dz], dq_got.at[dz], ctx_at(nz - dz, 0, 0), tp)
-    for dl in range(nl):
-        tp_sides(dkv_all, got_all, dl)
-    if nl > 1:
-        got_all[0, 1].wait_recv()
-
-    def term(s, weights):
-        return matmul_nt(dkv_all[s], weights).astype(jnp.bfloat16).astype(jnp.float32)
-
+    tp_sides(dkv_all, got_all, 0)
     for s in got_w_sib:
         got_w_sib[s].wait_recv()
-    d_input = term(0, wkv[pl.ds(pl.multiple_of(tp * WIDE, WIDE), WIDE), :])
+
+    def term(dx, dl):
+        if dx == 0:
+            weights = wkv[pl.ds(pl.multiple_of(tp_at(0, dl) * WIDE, WIDE), WIDE), :]
+        else:
+            weights = w_cols[dx * nl + dl]
+        return matmul_nt(dkv_all[dx * nl], weights).astype(jnp.bfloat16).astype(jnp.float32)
+
+    def near_terms(dl):
+        total = term(0, dl)
+        for dx in beside(nx):
+            total += term(dx, dl)
+        return total
+
+    sums = [near_terms(dl) for dl in reversed(range(nl))]
+    if nx == 4:
+        tp_opposite(got_all, 0)
     if nl > 1:
-        d_input += term(1, w_cols[1])
-    for dx in beside(nx):
-        d_input += term(dx * nl, w_cols[dx * nl])
-    if nl > 1:
-        for dx in beside(nx):
-            d_input += term(dx * nl + 1, w_cols[dx * nl + 1])
-    if nx == 4:
-        for dl in range(nl):
-            tp_opposite(got_all, dl)
-            d_input += term(2 * nl + dl, w_cols[2 * nl + dl])
-    di_res[...] = d_input.astype(jnp.bfloat16)
-    store_di = local(di_res, di_out)
+        di_snd[...] = (sums[0] + term(2, 1) if nx == 4 else sums[0]).astype(jnp.bfloat16)
+        got_di = remote(di_snd, di_got, ctx, tp_at(0, 1))
+    d_input = sums[-1] + term(2, 0) if nx == 4 else sums[-1]
 
     d_query = both_cores(0)
     for dz in beside(nz):
@@ -498,6 +556,12 @@
         cols = slice(h * HD, (h + 1) * HD)
         dq_res[:, cols] = d_query[:, cols].T.astype(jnp.bfloat16)
     store_dq = local(dq_res, dq_out)
+
+    if nl > 1:
+        got_di.wait_recv()
+        d_input += di_got[...].astype(jnp.float32)
+    di_res[...] = d_input.astype(jnp.bfloat16)
+    store_di = local(di_res, di_out)
     for copy in sent:
         copy.wait_send()
     store_dq.wait()
@@ -510,7 +574,7 @@
     bf16, f32 = jnp.bfloat16, jnp.float32
     half = ROPE_BASE ** (-(np.arange(HD // 2) * 2.0) / HD)
     freq = jnp.asarray(np.concatenate([half, half])[None, :].astype(np.float32))
-    copies = 128
+    copies = 160
     vmem = pltpu.VMEM
     hbm = pl.BlockSpec(memory_space=pl.ANY)
     flops = 2 * nj * WIDE * ny * ROWS * HD * 5
@@ -540,6 +604,7 @@
             vmem((2, nz, WIDE), f32),
             vmem((nj, 2, nz, WIDE), f32),
             vmem((nj, 1, WIDE), f32),
+            vmem((nj, 2 * ROWS, WIDE), f32),
             vmem((nj, HD, WIDE), f32),
             vmem((2 * nz, HD, WIDE), bf16),
             vmem((nz, HD, WIDE), bf16),
@@ -553,6 +618,8 @@
             vmem((nt, WIDE, 2 * HD), bf16),
             vmem((ROWS, WIDE), bf16),
             vmem((ROWS, WIDE), bf16),
+            vmem((ROWS, WIDE), bf16),
+            vmem((ROWS, WIDE), bf16),
             pltpu.SemaphoreType.DMA((copies,)),
             pltpu.SemaphoreType.DMA((copies,)),
             pltpu.SemaphoreType.DMA((8,)),

time: 83.8 us -> 78.2 us (0.933); the launches traced: 82.5 us -> 78 us
  Pallas kernels: 79.6 us -> 75.1 us
    pallas_call x1, Pallas kernels: 79.6 us -> 75.1 us  [body(): pl.pallas_call(functools.partial(kernel, grid), out_shape=(jax.ShapeDtype...]
where the time goes in v4:
time: 78.2 us; the launch traced here: 78 us
  Pallas kernels  75.1 us (96%)
  local copies, waits for them, and re-layouts  2.26 us (3%)
    pallas_call x1, Pallas kernels, body(): pl.pallas_call(functools.partial(kernel, grid), out_shape=(jax.ShapeDtype...  75.1 us
    unnamed x4, local copies, waits for them, and re-layouts  2.26 us

profile of v4, /device:TPU:1, one launch (start us, length us, event | category | flops | bytes accessed | tf_op | source)
XLA Modules:
  0.0 78.0 jit_solution(1575954845216806374)
XLA Ops:
  0.6 75.1 %shard_map.95 = (bf16[128,512]{1,0:T(8,128)(2,1)}, bf16[128,512]{1,0:T(8,128)(2,1)}) custom-call(bf16[128,512]{1,0:T(8,128)(2,1)} %x_in.1, bf16[4096,128]{1,0:T(8,128)(2,1)} %wk_in.1, bf16[4096,128]{1,0:T(8,128)(2,1)} %wv_in.1, bf16[128,512]{1,0:T(8,128)(2,1)} %q_in.1, bf16[128,512]{1,0:T(8,128)(2,1)} %o_in.1, bf16[128,512]{1,0:T(8,128)(2,1)} %g_in.1, ...), custom_call_target="tpu_custom_call" | custom-call | flops 5368709120 | bytes 4194304 | tf_op jit(solution)/shard_map/pallas_call | solution.py:581
  75.7 0.0 copy-start
  75.8 1.6 %copy.12 = bf16[128,512]{1,0:T(8,128)(2,1)} copy(bf16[128,512]{1,0:T(8,128)(2,1)} %get-tuple-element.4) | data formatting | bytes 262144
  77.4 0.0 copy-done
  77.4 0.7 copy.13
Async XLA Ops:
  75.7 1.6 %copy-start = (bf16[128,512]{1,0:T(8,128)(2,1)S(1)}, bf16[128,512]{1,0:T(8,128)(2,1)}, u32[]{:S(2)}) copy-start(bf16[128,512]{1,0:T(8,128)(2,1)} %get-tuple-element.5) | copy-start | bytes 393220

commit v5 on v4

--- a/solution.py
+++ b/solution.py
@@ -52,7 +52,7 @@
     grid, x_in, wk_in, wv_in, q_in, o_in, g_in, roster, freq,
     dq_out, di_out,
     xg, wkv, qg, gg, ol, kv, kt, posk, posq, probs, peak, total, fac, lse_own, lse_got,
-    delta, ahead, dqt, dq_snd, dq_sib, dq_half, dq_got, acc, dkv_snd, dkv_relay, dkv_got, dkv_all, w_cols, di_snd, di_got, dq_res, di_res,
+    delta, ahead, dqt, dq_snd, dq_sib, dq_half, dq_got, acc, held, dkv_snd, dkv_relay, dkv_got, dkv_all, w_cols, di_snd, di_got,
     send_sem, recv_sem, local_sem,
 ):
     nz, ny, nx, nl = grid
@@ -127,14 +127,19 @@
     def tp_begin(src, buf):
         got = {}
         if nl > 1:
-            got[0, 1] = remote(src, buf.at[1], ctx, tp_at(0, 1))
+            for turn, part in enumerate((low, high)):
+                got[0, 1, turn] = remote(src.at[part, :], buf.at[1, part, :], ctx, tp_at(0, 1))
         got.update(tp_round(src, buf, 0))
         return got
 
     def tp_partner(buf, got):
         if nl > 1:
-            got[0, 1].wait_recv()
-            got.update(tp_round(buf.at[1], buf, 1))
+            for turn, part in enumerate((low, high)):
+                got[0, 1, turn].wait_recv()
+                for dx in beside(nx):
+                    got[dx, 1, turn if halves(dx)[0] is low else 1 - turn] = remote(
+                        buf.at[1, part, :], buf.at[dx * nl + 1, part, :], ctx, tp_at(dx, 0)
+                    )
 
     def tp_sides(buf, got, dl):
         for dx in beside(nx):
@@ -223,8 +228,12 @@
     load_wv.wait()
     raw = project(0, 0)
 
+    if nl > 1:
+        for turn in range(2):
+            got_x[0, 1, turn].wait_send()
+            sent.remove(got_x[0, 1, turn])
+    got_q = z_begin(q_in, qg)
     tp_partner(xg, got_x)
-    got_q = z_begin(q_in, qg)
     tp_sides(xg, got_x, 0)
     if nl > 1:
         raw += project(0, 1)
@@ -338,8 +347,10 @@
     mine = pl.ds(pl.multiple_of(c * HD, HD), HD)
     got_w = {}
 
+    blocks = [(dx, dl) for dl in reversed(range(nl)) for dx in range(1, nx)]
+
     def send_weights():
-        for dx, dl in [(dx, dl) for dl in reversed(range(nl)) for dx in range(1, nx)]:
+        for dx, dl in blocks:
             rows = pl.ds(pl.multiple_of(tp_at(dx, dl) * WIDE, WIDE), WIDE)
             s = dx * nl + dl
             got_w[s] = remote(wkv.at[rows, mine], w_cols.at[s, :, mine], ctx, tp_at(dx, 0))
@@ -401,10 +412,12 @@
         copy.wait_recv()
     z_finish(got_g)
 
-    def first_d_probs(j):
-        ahead[j] = matmul_nt(kv[0:2 * ROWS, HD:2 * HD], stacked(gg[j])) - delta[j]
-
-    each(nj, first_d_probs)
+    def first_d_probs(k, j):
+        rows = slice(2 * k * ROWS, 2 * (k + 1) * ROWS)
+        ahead[k, j] = matmul_nt(kv[rows, HD:2 * HD], stacked(gg[j])) - delta[j]
+
+    for k in range(min(2, chunks)):
+        each(nj, functools.partial(first_d_probs, k))
     take_totals(0, got_lse[0])
 
     got_dkv = {}
@@ -427,14 +440,29 @@
         src = dkv_snd.at[place[dy], pl.ds(start, count), :]
         return remote(src, dst.at[pl.ds(start, count), :], ctx_at(0, (ny + to) % ny, 0), tp)
 
+    def send_held():
+        if ny != 8:
+            return
+        for i, (dy, half) in enumerate(((2, low), (6, high))):
+            p = place[dy]
+            got_relay[dy].wait_recv()
+            got_relay[4, dy].wait_recv()
+            part = held[i] + dkv_relay[i].astype(jnp.float32)
+            rest = high if half is low else low
+            dkv_snd[p, half, :] = (
+                part[half] + dkv_relay[2, half, :].astype(jnp.float32)
+            ).astype(jnp.bfloat16)
+            dkv_snd[p, rest, :] = part[rest].astype(jnp.bfloat16)
+            got_dkv[dy] = dkv_send(dy, -dy, dkv_got.at[p])
+
     for k in range(chunks):
         rows = slice(2 * k * ROWS, 2 * (k + 1) * ROWS)
         acc[...] = jnp.zeros_like(acc)
 
         def grad_step(j, k=k, rows=rows):
             gs, qs = stacked(gg[j]), stacked(qg[j])
-            if k == 0:
-                d_probs = ahead[j]
+            if k < 2:
+                d_probs = ahead[k, j]
             else:
                 d_probs = matmul_nt(kv[rows, HD:2 * HD], gs) - delta[j]
             prob = probs[k, j] * fac[k, place_of(j)]
@@ -456,17 +484,12 @@
         if k == chunks - 1:
             if k:
                 each(nz, lambda i, step=grad_step: step(2 * i + 1))
+            send_held()
             for dz in far_first(nz):
                 dq_snd[dz] = (dqt[2 * dz + 1] * SCALE).astype(jnp.bfloat16)
                 got_sib[dz] = remote(dq_snd.at[dz], dq_sib.at[dz], ctx_at(0, 0, 1), tp)
             if k:
-                for dz in [dz for dz in (2, 1) if dz < nz]:
-                    grad_step(2 * dz)
-                send_halves()
-                for dz in [dz for dz in (3, 0) if dz < nz]:
-                    grad_step(2 * dz)
-            else:
-                send_halves()
+                each(nz, lambda i, step=grad_step: step(2 * i))
         for i, dy in enumerate(order[2 * k:2 * k + 2]):
             if dy == 0:
                 continue
@@ -474,16 +497,9 @@
             part = acc[i * ROWS:(i + 1) * ROWS, :]
             d_key, d_value = part[:, 0:HD] * SCALE, part[:, HD:2 * HD]
             if ny == 8 and dy in (2, 6):
-                side, half = (0, low) if dy == 2 else (1, high)
-                got_relay[dy].wait_recv()
-                got_relay[4, dy].wait_recv()
-                d_key += dkv_relay[side, :, 0:HD].astype(jnp.float32)
-                d_value += dkv_relay[side, :, HD:2 * HD].astype(jnp.float32)
-                more = dkv_relay[2, half, :].astype(jnp.float32)
-                none = jnp.zeros_like(more)
-                more = jnp.concatenate([more, none] if dy == 2 else [none, more], axis=0)
-                d_key += more[:, 0:HD]
-                d_value += more[:, HD:2 * HD]
+                held[i, :, 0:HD] = d_key
+                held[i, :, HD:2 * HD] = d_value
+                continue
             dkv_snd[p, :, 0:HD] = d_key.astype(jnp.bfloat16)
             dkv_snd[p, :, HD:2 * HD] = d_value.astype(jnp.bfloat16)
             if ny == 8 and dy == 4:
@@ -496,6 +512,8 @@
                 got_dkv[dy] = dkv_send(dy, -dy, dkv_got.at[p])
         if k == max(chunks - 2, 0):
             share_weights()
+        if k == chunks - 1:
+            send_halves()
 
     i = own % 2
     d_key = acc[i * ROWS:(i + 1) * ROWS, 0:HD] * SCALE
@@ -554,18 +572,14 @@
         d_query += dq_got[dz].astype(jnp.float32)
     for h in range(GROUP):
         cols = slice(h * HD, (h + 1) * HD)
-        dq_res[:, cols] = d_query[:, cols].T.astype(jnp.bfloat16)
-    store_dq = local(dq_res, dq_out)
+        dq_out[:, cols] = d_query[:, cols].T.astype(jnp.bfloat16)
 
     if nl > 1:
         got_di.wait_recv()
         d_input += di_got[...].astype(jnp.float32)
-    di_res[...] = d_input.astype(jnp.bfloat16)
-    store_di = local(di_res, di_out)
+    di_out[...] = d_input.astype(jnp.bfloat16)
     for copy in sent:
         copy.wait_send()
-    store_dq.wait()
-    store_di.wait()
 
 
 def body(grid, x_stash, w_key, w_value, query, out_stash, d_out, roster):
@@ -580,13 +594,10 @@
     flops = 2 * nj * WIDE * ny * ROWS * HD * 5
     return pl.pallas_call(
         functools.partial(kernel, grid),
-        out_shape=(
-            jax.ShapeDtypeStruct((ROWS, WIDE), bf16),
-            jax.ShapeDtypeStruct((ROWS, WIDE), bf16),
-        ),
+        out_shape=(vmem((ROWS, WIDE), bf16), vmem((ROWS, WIDE), bf16)),
         in_specs=[hbm] * 6
         + [pl.BlockSpec(memory_space=pltpu.SMEM), pl.BlockSpec(memory_space=pltpu.VMEM)],
-        out_specs=(hbm, hbm),
+        out_specs=(pl.BlockSpec(memory_space=vmem), pl.BlockSpec(memory_space=vmem)),
         scratch_shapes=[
             vmem((nt, ROWS, WIDE), bf16),
             vmem((nt * WIDE, 2 * HD), bf16),
@@ -604,20 +615,19 @@
             vmem((2, nz, WIDE), f32),
             vmem((nj, 2, nz, WIDE), f32),
             vmem((nj, 1, WIDE), f32),
-            vmem((nj, 2 * ROWS, WIDE), f32),
+            vmem((min(2, chunks), nj, 2 * ROWS, WIDE), f32),
             vmem((nj, HD, WIDE), f32),
             vmem((2 * nz, HD, WIDE), bf16),
             vmem((nz, HD, WIDE), bf16),
             vmem((HD, WIDE), bf16),
             vmem((nz, HD, WIDE), bf16),
             vmem((2 * ROWS, 2 * HD), f32),
+            vmem((2, ROWS, 2 * HD), f32),
             vmem((ny, ROWS, 2 * HD), bf16),
             vmem((3, ROWS, 2 * HD), bf16),
             vmem((ny, ROWS, 2 * HD), bf16),
             vmem((nt, ROWS, 2 * HD), bf16),
             vmem((nt, WIDE, 2 * HD), bf16),
-            vmem((ROWS, WIDE), bf16),
-            vmem((ROWS, WIDE), bf16),
             vmem((ROWS, WIDE), bf16),
             vmem((ROWS, WIDE), bf16),
             pltpu.SemaphoreType.DMA((copies,)),

time: 78.2 us -> 75.5 us (0.965)
  Pallas kernels: 75.1 us -> 73.4 us
  local copies, waits for them, and re-layouts: 2.26 us -> 1.31 us
    pallas_call x1, Pallas kernels: 75.1 us -> 73.4 us  [body(): pl.pallas_call(functools.partial(kernel, grid), out_shape=(vmem((ROWS, WI...]
    unnamed x4 -> x2, local copies, waits for them, and re-layouts: 2.26 us -> 1.31 us
where the time goes in v5:
time: 75.5 us; the launch traced here: 75.3 us
  Pallas kernels  73.4 us (97%)
  local copies, waits for them, and re-layouts  1.31 us (2%)
    pallas_call x1, Pallas kernels, body(): pl.pallas_call(functools.partial(kernel, grid), out_shape=(vmem((ROWS, WI...  73.4 us

profile of v5, /device:TPU:1, one launch (start us, length us, event | category | flops | bytes accessed | tf_op | source)
XLA Modules:
  0.0 75.3 jit_solution(12522593074698798205)
XLA Ops:
  0.6 73.4 %shard_map.95 = (bf16[128,512]{1,0:T(8,128)(2,1)S(1)}, bf16[128,512]{1,0:T(8,128)(2,1)S(1)}) custom-call(bf16[128,512]{1,0:T(8,128)(2,1)} %x_in.1, bf16[4096,128]{1,0:T(8,128)(2,1)} %wk_in.1, bf16[4096,128]{1,0:T(8,128)(2,1)} %wv_in.1, bf16[128,512]{1,0:T(8,128)(2,1)} %q_in.1, bf16[128,512]{1,0:T(8,128)(2,1)} %o_in.1, bf16[128,512]{1,0:T(8,128)(2,1)} %g_in.1, ...), custom_call_target="tpu_custom_call" | custom-call | flops 5368709120 | bytes 4194304 | tf_op jit(solution)/shard_map/pallas_call | solution.py:595
  74.0 0.7 copy.12
  74.7 0.7 copy.13

commit v6 on v5

--- a/solution.py
+++ b/solution.py
@@ -93,19 +93,19 @@
         sent.append(copy)
         return copy
 
+    barrier = pltpu.get_barrier_semaphore()
+    partners = [(ctx, tp_at(dx, dl)) for dx, dl in tp_peers]
+    partners += [(ctx_at(dz, 0, dc), tp) for dz, dc in q_peers]
+    partners += [(ctx_at(0, dy, 0), tp) for dy in direct]
+    for partner in partners:
+        pl.semaphore_signal(barrier, inc=1, device_id=partner, device_id_type=pl.DeviceIdType.MESH)
+
     load_x = local(x_in, xg.at[0])
     load_wk = local(wk_in, wkv.at[:, 0:HD])
     load_wv = local(wv_in, wkv.at[:, HD:2 * HD])
     load_g = local(g_in, gg.at[0])
     load_o = local(o_in, ol)
     load_q = local(q_in, qg.at[0])
-
-    barrier = pltpu.get_barrier_semaphore()
-    partners = [(ctx, tp_at(dx, dl)) for dx, dl in tp_peers]
-    partners += [(ctx_at(dz, 0, dc), tp) for dz, dc in q_peers]
-    partners += [(ctx_at(0, dy, 0), tp) for dy in direct]
-    for partner in partners:
-        pl.semaphore_signal(barrier, inc=1, device_id=partner, device_id_type=pl.DeviceIdType.MESH)
 
     pl.semaphore_wait(barrier, len(partners))
 
@@ -186,10 +186,6 @@
             for dz in beside(nz):
                 got[2, 0, dz].wait_recv()
             got[2, 1] = remote(buf.at[4], buf.at[5], ctx_at(0, 0, 1), tp)
-
-    def z_finish(got):
-        for dz in range(nz):
-            got[dz, 1].wait_recv()
 
     got_x = tp_begin(x_in, xg)
 
@@ -410,14 +406,23 @@
         kt[k] = kv[rows, 0:HD].astype(jnp.float32).T.astype(jnp.bfloat16)
     for copy in got_delta:
         copy.wait_recv()
-    z_finish(got_g)
-
-    def first_d_probs(k, j):
-        rows = slice(2 * k * ROWS, 2 * (k + 1) * ROWS)
-        ahead[k, j] = matmul_nt(kv[rows, HD:2 * HD], stacked(gg[j])) - delta[j]
-
-    for k in range(min(2, chunks)):
-        each(nj, functools.partial(first_d_probs, k))
+
+    def first_d_probs(slots):
+        def run(k, carry):
+            rows = pl.ds(pl.multiple_of(k * 2 * ROWS, 2 * ROWS), 2 * ROWS)
+            for j in slots:
+                ahead[k, j] = matmul_nt(kv[rows, HD:2 * HD], stacked(gg[j])) - delta[j]
+            return carry
+
+        lax.fori_loop(0, chunks, run, 0)
+
+    got_g[0, 1].wait_recv()
+    for dz in beside(nz):
+        got_g[dz, 1].wait_recv()
+    first_d_probs(early)
+    if late:
+        got_g[2, 1].wait_recv()
+        first_d_probs(late)
     take_totals(0, got_lse[0])
 
     got_dkv = {}
@@ -461,12 +466,8 @@
 
         def grad_step(j, k=k, rows=rows):
             gs, qs = stacked(gg[j]), stacked(qg[j])
-            if k < 2:
-                d_probs = ahead[k, j]
-            else:
-                d_probs = matmul_nt(kv[rows, HD:2 * HD], gs) - delta[j]
             prob = probs[k, j] * fac[k, place_of(j)]
-            d_scores = (prob * d_probs).astype(jnp.bfloat16)
+            d_scores = (prob * ahead[k, j]).astype(jnp.bfloat16)
             acc[:, HD:2 * HD] += matmul(prob.astype(jnp.bfloat16), gs)
             acc[:, 0:HD] += matmul(d_scores, qs)
             part = matmul(kt[k], d_scores)
@@ -482,14 +483,20 @@
         if 0 < k < chunks - 1:
             each(nj, grad_step)
         if k == chunks - 1:
-            if k:
-                each(nz, lambda i, step=grad_step: step(2 * i + 1))
-            send_held()
-            for dz in far_first(nz):
-                dq_snd[dz] = (dqt[2 * dz + 1] * SCALE).astype(jnp.bfloat16)
-                got_sib[dz] = remote(dq_snd.at[dz], dq_sib.at[dz], ctx_at(0, 0, 1), tp)
-            if k:
-                each(nz, lambda i, step=grad_step: step(2 * i))
+            for some in ((2,), (1, 3), (0,)):
+                some = [dz for dz in some if dz < nz]
+                for dz in some:
+                    if k:
+                        grad_step(2 * dz + 1)
+                for dz in some:
+                    dq_snd[dz] = (dqt[2 * dz + 1] * SCALE).astype(jnp.bfloat16)
+                    got_sib[dz] = remote(dq_snd.at[dz], dq_sib.at[dz], ctx_at(0, 0, 1), tp)
+                for dz in some:
+                    if k:
+                        grad_step(2 * dz)
+                if (0 if nz == 1 else 1) in some:
+                    send_held()
+                    send_halves()
         for i, dy in enumerate(order[2 * k:2 * k + 2]):
             if dy == 0:
                 continue
@@ -512,20 +519,6 @@
                 got_dkv[dy] = dkv_send(dy, -dy, dkv_got.at[p])
         if k == max(chunks - 2, 0):
             share_weights()
-        if k == chunks - 1:
-            send_halves()
-
-    i = own % 2
-    d_key = acc[i * ROWS:(i + 1) * ROWS, 0:HD] * SCALE
-    d_value = acc[i * ROWS:(i + 1) * ROWS, HD:2 * HD]
-    for dy in got_dkv:
-        got_dkv[dy].wait_recv()
-        d_key += dkv_got[place[dy], :, 0:HD].astype(jnp.float32)
-        d_value += dkv_got[place[dy], :, HD:2 * HD].astype(jnp.float32)
-    d_key = d_key * cosine - pltpu.roll(d_key, HD // 2, 1) * sine
-    d_kv = jnp.concatenate([d_key, d_value], axis=1).astype(jnp.bfloat16)
-    dkv_all[0] = d_kv
-    got_all = tp_round(dkv_all.at[0], dkv_all, 0)
 
     got_dq = {}
     for dz in beside(nz):
@@ -541,7 +534,24 @@
         else:
             dq_snd[nz + dz] = both.astype(jnp.bfloat16)
         got_dq[dz] = remote(dq_snd.at[nz + dz], dq_got.at[dz], ctx_at(nz - dz, 0, 0), tp)
-    tp_sides(dkv_all, got_all, 0)
+
+    i = own % 2
+    d_key = acc[i * ROWS:(i + 1) * ROWS, 0:HD] * SCALE
+    d_value = acc[i * ROWS:(i + 1) * ROWS, HD:2 * HD]
+    for dy in got_dkv:
+        got_dkv[dy].wait_recv()
+        d_key += dkv_got[place[dy], :, 0:HD].astype(jnp.float32)
+        d_value += dkv_got[place[dy], :, HD:2 * HD].astype(jnp.float32)
+    d_key = d_key * cosine - pltpu.roll(d_key, HD // 2, 1) * sine
+    d_kv = jnp.concatenate([d_key, d_value], axis=1).astype(jnp.bfloat16)
+    dkv_all[0] = d_kv
+    got_all = [
+        remote(dkv_all.at[0], dkv_all.at[dx * nl], ctx, tp_at(dx, 0))
+        for dx in beside(nx) + ([2] if nx == 4 else [])
+    ]
+
+    for copy in got_all[:2]:
+        copy.wait_recv()
     for s in got_w_sib:
         got_w_sib[s].wait_recv()
 
@@ -559,8 +569,8 @@
         return total
 
     sums = [near_terms(dl) for dl in reversed(range(nl))]
-    if nx == 4:
-        tp_opposite(got_all, 0)
+    for copy in got_all[2:]:
+        copy.wait_recv()
     if nl > 1:
         di_snd[...] = (sums[0] + term(2, 1) if nx == 4 else sums[0]).astype(jnp.bfloat16)
         got_di = remote(di_snd, di_got, ctx, tp_at(0, 1))
@@ -615,7 +625,7 @@
             vmem((2, nz, WIDE), f32),
             vmem((nj, 2, nz, WIDE), f32),
             vmem((nj, 1, WIDE), f32),
-            vmem((min(2, chunks), nj, 2 * ROWS, WIDE), f32),
+            vmem((chunks, nj, 2 * ROWS, WIDE), f32),
             vmem((nj, HD, WIDE), f32),
             vmem((2 * nz, HD, WIDE), bf16),
             vmem((nz, HD, WIDE), bf16),

time: 75.5 us -> 74.9 us (level); the launches traced: 75.3 us -> 73.9 us
  Pallas kernels: 73.4 us -> 72 us
    pallas_call x1, Pallas kernels: 73.4 us -> 72 us  [body(): pl.pallas_call(functools.partial(kernel, grid), out_shape=(vmem((ROWS, WI...]
where the time goes in v6:
time: 74.9 us; the launch traced here: 73.9 us
  Pallas kernels  72 us (96%)
  local copies, waits for them, and re-layouts  1.31 us (2%)
    pallas_call x1, Pallas kernels, body(): pl.pallas_call(functools.partial(kernel, grid), out_shape=(vmem((ROWS, WI...  72 us

profile of v6, /device:TPU:1, one launch (start us, length us, event | category | flops | bytes accessed | tf_op | source)
XLA Modules:
  0.0 73.9 jit_solution(18026532090057481032)
XLA Ops:
  0.6 72.0 %shard_map.95 = (bf16[128,512]{1,0:T(8,128)(2,1)S(1)}, bf16[128,512]{1,0:T(8,128)(2,1)S(1)}) custom-call(bf16[128,512]{1,0:T(8,128)(2,1)} %x_in.1, bf16[4096,128]{1,0:T(8,128)(2,1)} %wk_in.1, bf16[4096,128]{1,0:T(8,128)(2,1)} %wv_in.1, bf16[128,512]{1,0:T(8,128)(2,1)} %q_in.1, bf16[128,512]{1,0:T(8,128)(2,1)} %o_in.1, bf16[128,512]{1,0:T(8,128)(2,1)} %g_in.1, ...), custom_call_target="tpu_custom_call" | custom-call | flops 5368709120 | bytes 4194304 | tf_op jit(solution)/shard_map/pallas_call | solution.py:605
  72.6 0.7 copy.12
  73.3 0.7 copy.13

commit v7 on v6

--- a/solution.py
+++ b/solution.py
@@ -331,7 +331,7 @@
                 fac[k, b * batch + i] = jnp.exp2(peak[k, b * batch + i] - lse[i:i + 1, :])
 
     def each(count, step):
-        unit = 4 if count % 4 == 0 else 1
+        unit = next(u for u in (8, 4, 1) if count % u == 0)
 
         def run(i, carry):
             for u in range(unit):
@@ -477,10 +477,8 @@
                 dqt[j] += part
 
         if k == 0:
-            each(batch, lambda a, step=grad_step: step(slot_of(a)))
             take_totals(1, got_lse[1])
-            each(batch, lambda a, step=grad_step: step(slot_of(batch + a)))
-        if 0 < k < chunks - 1:
+        if k < chunks - 1 or k == 0:
             each(nj, grad_step)
         if k == chunks - 1:
             for some in ((2,), (1, 3), (0,)):

time: 74.9 us -> 74 us (0.988)
  Pallas kernels: 72 us -> 70.7 us
    pallas_call x1, Pallas kernels: 72 us -> 70.7 us  [body(): pl.pallas_call(functools.partial(kernel, grid), out_shape=(vmem((ROWS, WI...]
where the time goes in v7:
time: 74 us; the launch traced here: 72.6 us
  Pallas kernels  70.7 us (96%)
  local copies, waits for them, and re-layouts  1.31 us (2%)
    pallas_call x1, Pallas kernels, body(): pl.pallas_call(functools.partial(kernel, grid), out_shape=(vmem((ROWS, WI...  70.7 us

profile of v7, /device:TPU:1, one launch (start us, length us, event | category | flops | bytes accessed | tf_op | source)
XLA Modules:
  0.0 72.6 jit_solution(9849613959589215924)
XLA Ops:
  0.6 70.7 %shard_map.95 = (bf16[128,512]{1,0:T(8,128)(2,1)S(1)}, bf16[128,512]{1,0:T(8,128)(2,1)S(1)}) custom-call(bf16[128,512]{1,0:T(8,128)(2,1)} %x_in.1, bf16[4096,128]{1,0:T(8,128)(2,1)} %wk_in.1, bf16[4096,128]{1,0:T(8,128)(2,1)} %wv_in.1, bf16[128,512]{1,0:T(8,128)(2,1)} %q_in.1, bf16[128,512]{1,0:T(8,128)(2,1)} %o_in.1, bf16[128,512]{1,0:T(8,128)(2,1)} %g_in.1, ...), custom_call_target="tpu_custom_call" | custom-call | flops 5368709120 | bytes 4194304 | tf_op jit(solution)/shard_map/pallas_call | solution.py:603
  71.3 0.7 copy.12
  72.0 0.7 copy.13
